TPU v7x, 128 devices: a whole 4x4x4 slice. The times are simulated.
128 devices in a mesh: row: 8 (over y_hi, x), col: 16 (over z, y_lo, core).
Axes of the slice: x: 4, y: 4 (y_hi: 2, y_lo: 2; y = y_hi * 2 + y_lo), z: 4, core: 2. Of those that a mesh axis runs over, the one named last changes fastest.
Arguments:
- weight: bfloat16 [14336, 53248], P(('row', 'col')), may hold values from -0.046875 to 0.046875
- start: float32 [53248, 64], P(('col', 'row')), may hold values from -6 to 6
Outputs:
- adapter_left: float32 [14336, 128], P(('row', 'col'))
- adapter_right: float32 [53248, 128], P(('col', 'row'))
- residual_weight: bfloat16 [14336, 53248], P(None, ('col', 'row'))
All inputs are finite; a program needn't handle non-finite values.
Results may differ from a plain program's by a relative error of at most 0.01155.
Values may be sent and summed in bfloat16 or wider, within the bound.
A program may use at most 128 MiB of HBM per device.

v0:
```python
import jax
import jax.numpy as jnp
from jax import lax
from jax.sharding import PartitionSpec as P

STEPS = 3
RANK = 128
SWEEPS = 4


HIGHEST = lax.Precision.HIGHEST


def product(left_side, right_side):
    return jnp.dot(left_side, right_side, precision=HIGHEST, preferred_element_type=jnp.float32)


def inner_product(left_side, right_side):
    return lax.dot_general(
        left_side,
        right_side,
        (((0,), (0,)), ((), ())),
        precision=HIGHEST,
        preferred_element_type=jnp.float32,
    )


def finish(cleaned, gram_matrix):
    factor = jnp.linalg.cholesky(gram_matrix)
    return jax.scipy.linalg.solve_triangular(factor, cleaned.T, lower=True).T


def extend(matrix, earlier, summer):
    if earlier is None:
        return finish(matrix, summer(inner_product(matrix, matrix)))
    coefficients = summer(inner_product(earlier, matrix))
    cleaned = matrix - product(earlier, coefficients)
    return finish(cleaned, summer(inner_product(cleaned, cleaned)))


def sum_everywhere(values):
    return lax.psum(values, ("row", "col"))


def small_subspace(gram_matrix):
    subspace_basis = jnp.eye(gram_matrix.shape[0], dtype=jnp.float32)[:, :RANK]
    for sweep_index in range(SWEEPS):
        grown = product(gram_matrix, subspace_basis)
        subspace_basis = finish(grown, inner_product(grown, grown))
    return subspace_basis


def shards(weight, start):
    weight_tile = lax.all_to_all(weight, "col", split_axis=1, concat_axis=0, tiled=True)
    left_list = []
    image_list = []
    right_list = [extend(start, None, sum_everywhere)]
    for turn_index in range(STEPS):
        low_right = right_list[-1].astype(jnp.bfloat16)
        whole_right = lax.all_gather(low_right, "row", axis=0, tiled=True)
        image_block = lax.psum_scatter(
            jnp.dot(weight_tile, whole_right, preferred_element_type=jnp.float32),
            "col",
            scatter_dimension=0,
            tiled=True,
        )
        earlier = jnp.concatenate(left_list, 1) if left_list else None
        left_list.append(extend(image_block, earlier, sum_everywhere))
        low_left = left_list[-1].astype(jnp.bfloat16)
        partial_back = lax.dot_general(
            weight_tile,
            lax.all_gather(low_left, "col", axis=0, tiled=True),
            (((0,), (0,)), ((), ())),
            preferred_element_type=jnp.float32,
        )
        back_block = lax.psum_scatter(partial_back, "row", scatter_dimension=0, tiled=True)
        image_list.append(back_block)
        if turn_index + 1 < STEPS:
            right_list.append(extend(back_block, jnp.concatenate(right_list, 1), sum_everywhere))
    krylov = jnp.concatenate(image_list, 1)
    subspace_basis = small_subspace(sum_everywhere(inner_product(krylov, krylov)))
    left_factor = product(jnp.concatenate(left_list, 1), subspace_basis)
    right_factor = product(krylov, subspace_basis)
    low_left = left_factor.astype(jnp.bfloat16)
    low_right = right_factor.astype(jnp.bfloat16)
    left_block = lax.all_gather(low_left, "col", axis=0, tiled=True)
    right_block = lax.all_gather(low_right, "row", axis=0, tiled=True)
    update = lax.dot_general(
        left_block, right_block, (((1,), (1,)), ((), ())), preferred_element_type=jnp.float32
    )
    residual_tile = (weight_tile.astype(jnp.float32) - update).astype(jnp.bfloat16)
    residual_weight = lax.all_to_all(residual_tile, "row", split_axis=1, concat_axis=0, tiled=True)
    return (left_factor, right_factor, residual_weight)


def solution(mesh):
    return jax.shard_map(
        shards,
        mesh=mesh,
        in_specs=(P(("row", "col"), None), P(("col", "row"), None)),
        out_specs=(P(("row", "col"), None), P(("col", "row"), None), P(None, ("col", "row"))),
        check_vma=False,
    )
```

profile of v0, /device:TPU:1, one launch (start us, length us, event | category | flops | bytes accessed | tf_op | source)
XLA Modules:
  0.0 1953.1 jit_solution(8662079051299740106)
XLA Ops:
  25.5 187.7 %psum.77 = f32[64,64]{0,1:T(8,128)S(1)} all-reduce(f32[64,64]{0,1:T(8,128)S(1)} %fusion.77), channel_id=1, replica_groups=mesh['row'=8,'col'=16] {'row','col'}, use_global_device_ids=true, to_apply=%region_0.0 | all-reduce | flops 4096 | bytes 32768 | tf_op jit(solution)/shard_map/psum | solution.py:42
  225.8 29.0 %all-gather = bf16[8,416,64]{1,2,0:T(8,128)(2,1)S(1)} all-gather(bf16[1,416,64]{1,2,0:T(8,128)(2,1)S(1)} %convert_bitcast_fusion.1), channel_id=1, replica_groups=mesh['row'=8,'col'=16] {'row'}, dimensions={0}, use_global_device_ids=true | all-gather | bytes 479232 | tf_op jit(solution)/shard_map/all_gather | solution.py:60
  265.2 61.0 %reduce-scatter.19.cloned.1.call-done = f32[112,64]{1,0:T(8,128)} async-done(((f32[1792,64]{1,0:T(8,128)}), f32[112,64]{1,0:T(8,128)}) %reduce-scatter.19.cloned.1.call-update) | async-done | bytes 28688
  327.3 68.0 %psum.78 = f32[64,64]{0,1:T(8,128)S(1)} all-reduce(f32[64,64]{0,1:T(8,128)S(1)} %fusion.78), channel_id=1, replica_groups=mesh['row'=8,'col'=16] {'row','col'}, use_global_device_ids=true, to_apply=%region_4.7 | all-reduce | flops 4096 | bytes 32768 | tf_op jit(solution)/shard_map/psum | solution.py:42
  408.6 19.3 all-gather.1
  436.7 69.1 %reduce-scatter.21.cloned.1.call-done = f32[416,64]{1,0:T(8,128)} async-done(((f32[3328,64]{1,0:T(8,128)}), f32[416,64]{1,0:T(8,128)}) %reduce-scatter.21.cloned.1.call-update) | async-done | bytes 106512
  507.0 65.6 %psum.79 = f32[64,64]{1,0:T(8,128)S(1)} all-reduce(f32[64,64]{1,0:T(8,128)S(1)} %fusion.79), channel_id=1, replica_groups=mesh['row'=8,'col'=16] {'row','col'}, use_global_device_ids=true, to_apply=%region_6.0 | all-reduce | flops 4096 | bytes 32768 | tf_op jit(solution)/shard_map/psum | solution.py:42
  574.3 63.0 %psum.80 = f32[64,64]{0,1:T(8,128)S(1)} all-reduce(f32[64,64]{0,1:T(8,128)S(1)} %fusion.80), channel_id=1, replica_groups=mesh['row'=8,'col'=16] {'row','col'}, use_global_device_ids=true, to_apply=%region_7.0 | all-reduce | flops 4096 | bytes 32768 | tf_op jit(solution)/shard_map/psum | solution.py:42
  649.8 29.0 %all-gather.2 = bf16[8,416,64]{1,2,0:T(8,128)(2,1)S(1)} all-gather(bf16[1,416,64]{1,2,0:T(8,128)(2,1)S(1)} %convert_bitcast_fusion), channel_id=1, replica_groups=mesh['row'=8,'col'=16] {'row'}, dimensions={0}, use_global_device_ids=true | all-gather | bytes 479232 | tf_op jit(solution)/shard_map/all_gather | solution.py:60
  689.1 60.6 %reduce-scatter.23.cloned.1.call-done = f32[112,64]{1,0:T(8,128)} async-done(((f32[1792,64]{1,0:T(8,128)}), f32[112,64]{1,0:T(8,128)}) %reduce-scatter.23.cloned.1.call-update) | async-done | bytes 28688
  750.7 67.9 %psum.81 = f32[64,64]{1,0:T(8,128)S(1)} all-reduce(f32[64,64]{1,0:T(8,128)S(1)} %fusion.81), channel_id=1, replica_groups=mesh['row'=8,'col'=16] {'row','col'}, use_global_device_ids=true, to_apply=%region_9.0 | all-reduce | flops 4096 | bytes 32768 | tf_op jit(solution)/shard_map/psum | solution.py:42
  820.0 62.9 %psum.82 = f32[64,64]{0,1:T(8,128)S(1)} all-reduce(f32[64,64]{0,1:T(8,128)S(1)} %fusion.82), channel_id=1, replica_groups=mesh['row'=8,'col'=16] {'row','col'}, use_global_device_ids=true, to_apply=%region_10.0 | all-reduce | flops 4096 | bytes 32768 | tf_op jit(solution)/shard_map/psum | solution.py:42
  923.1 70.0 %reduce-scatter.25.cloned.1.call-done = f32[416,64]{1,0:T(8,128)} async-done(((f32[3328,64]{1,0:T(8,128)}), f32[416,64]{1,0:T(8,128)}) %reduce-scatter.25.cloned.1.call-update) | async-done | bytes 106512
  994.6 65.6 %psum.83 = f32[128,64]{0,1:T(8,128)S(1)} all-reduce(f32[128,64]{0,1:T(8,128)S(1)} %fusion.3), channel_id=1, replica_groups=mesh['row'=8,'col'=16] {'row','col'}, use_global_device_ids=true, to_apply=%region_12.0 | all-reduce | flops 8192 | bytes 65536 | tf_op jit(solution)/shard_map/psum | solution.py:42
  1061.9 63.0 %psum.84 = f32[64,64]{0,1:T(8,128)S(1)} all-reduce(f32[64,64]{0,1:T(8,128)S(1)} %fusion.83), channel_id=1, replica_groups=mesh['row'=8,'col'=16] {'row','col'}, use_global_device_ids=true, to_apply=%region_13.0 | all-reduce | flops 4096 | bytes 32768 | tf_op jit(solution)/shard_map/psum | solution.py:42
  1137.4 29.4 %all-gather.4 = bf16[8,416,64]{1,2,0:T(8,128)(2,1)S(1)} all-gather(bf16[1,416,64]{1,2,0:T(8,128)(2,1)S(1)} %fusion), channel_id=1, replica_groups=mesh['row'=8,'col'=16] {'row'}, dimensions={0}, use_global_device_ids=true | all-gather | bytes 479232 | tf_op jit(solution)/shard_map/all_gather | solution.py:60
  1177.1 60.5 %reduce-scatter.27.cloned.1.call-done = f32[112,64]{1,0:T(8,128)} async-done(((f32[1792,64]{1,0:T(8,128)}), f32[112,64]{1,0:T(8,128)}) %reduce-scatter.27.cloned.1.call-update) | async-done | bytes 28688
  1238.7 68.1 %psum.85 = f32[128,64]{0,1:T(8,128)S(1)} all-reduce(f32[128,64]{0,1:T(8,128)S(1)} %fusion.41), channel_id=1, replica_groups=mesh['row'=8,'col'=16] {'row','col'}, use_global_device_ids=true, to_apply=%region_15.0 | all-reduce | flops 8192 | bytes 65536 | tf_op jit(solution)/shard_map/psum | solution.py:42
  1308.1 62.6 %psum.86 = f32[64,64]{0,1:T(8,128)S(1)} all-reduce(f32[64,64]{0,1:T(8,128)S(1)} %fusion.84), channel_id=1, replica_groups=mesh['row'=8,'col'=16] {'row','col'}, use_global_device_ids=true, to_apply=%region_16.0 | all-reduce | flops 4096 | bytes 32768 | tf_op jit(solution)/shard_map/psum | solution.py:42
  1411.0 70.0 %reduce-scatter.29.cloned.1.call-done = f32[416,64]{1,0:T(8,128)} async-done(((f32[3328,64]{1,0:T(8,128)}), f32[416,64]{1,0:T(8,128)}) %reduce-scatter.29.cloned.1.call-update) | async-done | bytes 106512
  1483.2 146.3 %all-reduce.2.cloned.1.call-done = f32[192,192]{1,0:T(8,128)} async-done(((f32[192,192]{1,0:T(8,128)}), f32[192,192]{1,0:T(8,128)}) %all-reduce.2.cloned.1.call-update) | async-done | bytes 147472 | tf_op jit(solution)/shard_map/psum | solution.py:42
  1732.2 20.8 %all_gather.30 = bf16[1792,128]{1,0:T(8,128)(2,1)S(1)} all-gather(bf16[112,128]{1,0:T(8,128)(2,1)S(1)} %get-tuple-element.6), channel_id=1, replica_groups=mesh['row'=8,'col'=16] {'col'}, dimensions={0}, use_global_device_ids=true | all-gather | bytes 487424 | tf_op jit(solution)/shard_map/all_gather | solution.py:86
  1752.9 30.2 %all_gather.31 = bf16[3328,128]{1,0:T(8,128)(2,1)S(1)} all-gather(bf16[416,128]{1,0:T(8,128)(2,1)S(1)} %get-tuple-element.10), channel_id=1, replica_groups=mesh['row'=8,'col'=16] {'row'}, dimensions={0}, use_global_device_ids=true | all-gather | bytes 958464 | tf_op jit(solution)/shard_map/all_gather | solution.py:87
  1808.6 132.2 %all_to_all.38 = bf16[1792,8,416]{0,2,1:T(8,128)(2,1)S(1)} all-to-all(bf16[1792,8,416]{0,2,1:T(8,128)(2,1)} %bitcast.241), channel_id=1, replica_groups=mesh['row'=8,'col'=16] {'row'}, dimensions={1} | all-to-all | bytes 23855104 | tf_op jit(solution)/shard_map/all_to_all | solution.py:92
  (166 shorter events, 336.1 us)
Async XLA Ops:
  7.2 18.1 copy-start
  17.4 238.4 %all-to-all-start = ((bf16[112,16,3328]{2,0,1:T(8,128)(2,1)}), bf16[112,16,3328]{2,0,1:T(8,128)(2,1)}, u32[]{:S(2)}, u32[]{:S(2)}) async-start(bf16[112,16,3328]{2,0,1:T(8,128)(2,1)} %bitcast.240), calls=%async_computation | async-start | bytes 23855104 | tf_op jit(solution)/shard_map/all_to_all | solution.py:54
  25.2 300.9 %reduce-scatter.19.cloned.1.call-start = ((), (), s32[]{:S(2)}) async-start(), calls=%async_computation.9 | async-start | bytes 974848
  265.1 240.7 %reduce-scatter.21.cloned.1.call-start = ((), (), s32[]{:S(2)}) async-start(), calls=%async_computation.10 | async-start | bytes 1916928
  436.7 313.1 %reduce-scatter.23.cloned.1.call-start = ((), (), s32[]{:S(2)}) async-start(), calls=%async_computation.11 | async-start | bytes 974848
  689.1 304.1 %reduce-scatter.25.cloned.1.call-start = ((), (), s32[]{:S(2)}) async-start(), calls=%async_computation.12 | async-start | bytes 1916928
  923.1 314.6 %reduce-scatter.27.cloned.1.call-start = ((), (), s32[]{:S(2)}) async-start(), calls=%async_computation.13 | async-start | bytes 974848
  1177.0 303.9 %reduce-scatter.29.cloned.1.call-start = ((), (), s32[]{:S(2)}) async-start(), calls=%async_computation.14 | async-start | bytes 1916928
  1410.8 218.7 %all-reduce.2.cloned.1.call-start = ((), (), s32[]{:S(2)}) async-start(), calls=%async_computation.8 | async-start | bytes 393216 | tf_op jit(solution)/shard_map/psum | solution.py:42
  1940.8 5.0 copy-start.1
Sparse Core Ops, SparseCore 0:
  265.2 60.8 reduce-scatter.18
  436.8 68.9 reduce-scatter.20
  689.2 60.4 reduce-scatter.22
  923.2 69.9 reduce-scatter.24
  1177.1 60.4 reduce-scatter.26
  1410.9 70.0 reduce-scatter.28
  1486.9 142.5 all-reduce.1
where the time goes:
time: 1970 us; the launch traced here: 1950 us
  blocking collectives  1100 us (56%)
  waiting for transfers between devices  538 us (27%)
  other arithmetic  164 us (8%)
  matrix products  74.3 us (4%)
  local copies, waits for them, and re-layouts  51.2 us (3%)
    psum x10, blocking collectives, sum_everywhere(): return lax.psum(values, ('row', 'col'))  774 us
    unnamed x13, waiting for transfers between devices  391 us
    psum x1, waiting for transfers between devices, sum_everywhere(): return lax.psum(values, ('row', 'col'))  146 us
    all_to_all x1, blocking collectives, shards(): lax.all_to_all(residual_tile, 'row', split_axis=1, concat_axis=0, tiled=T...  132 us
    another operation x30, other arithmetic, finish(): factor = jnp.linalg.cholesky(gram_matrix)  88.9 us
    all_gather x3, blocking collectives, shards(): whole_right = lax.all_gather(low_right, 'row', axis=0, tiled=True)  87.3 us
    another operation x20, other arithmetic, finish(): return jax.scipy.linalg.solve_triangular(factor, cleaned.T, lower=True).T  75.3 us
    all_gather x3, blocking collectives, shards(): lax.all_gather(low_left, 'col', axis=0, tiled=True)  57.1 us
  transfers between devices with their start and end apart: 8, of which 7 were waited for; matrix products, arithmetic and copies ran while one was open for 1% of the time, Pallas kernels for 0%

commit v1 on v0

v1 whole, which is shorter than its diff:
```python
import functools

import jax
import jax.numpy as jnp
from jax import lax
from jax.experimental import pallas as pl
from jax.experimental.pallas import tpu as pltpu
from jax.sharding import PartitionSpec as P

STEPS = 3
RANK = 128
SWEEPS = 4
B = 64
LANES = 128

NX, NYH, NYL, NZ, NC = 4, 2, 2, 4, 2
ROWS, COLS = 112, 416

HIGHEST = lax.Precision.HIGHEST
MESH = pl.DeviceIdType.MESH
F32 = jnp.float32
BF16 = jnp.bfloat16
NT = (((1,), (1,)), ((), ()))
NN = (((1,), (0,)), ((), ()))

RSC, RSZ, RSY, RSX, AGX, AGY, AGZ, AGC, ARC, ARZ, ARY, ARX, ARB = range(13)


def dot(left, right, dims=NN):
    return lax.dot_general(left, right, dims, precision=HIGHEST, preferred_element_type=F32)


def fast(left, right, dims=NN):
    return lax.dot_general(left, right, dims, preferred_element_type=F32)


def inverse_factor(gram):
    sub = lax.broadcasted_iota(jnp.int32, (B, 2 * B), 0)
    lane = lax.broadcasted_iota(jnp.int32, (B, 2 * B), 1)
    wide = jnp.concatenate([gram, jnp.zeros_like(gram)], 1)
    wide = jnp.where(lane == sub + B, 1.0, wide)

    def step(k, carry):
        wide, pivots = carry
        row = jnp.sum(jnp.where(sub == k, wide, 0.0), axis=0, keepdims=True)
        pivot = row[:, 0:1]
        scaled = row * (1.0 / pivot)
        column = jnp.where(sub[:, 0:1] > k, wide[:, 0:1], 0.0)
        wide = wide - column * scaled
        pivots = jnp.where(sub == k, pivot, pivots)
        return pltpu.roll(wide, 2 * B - 1, 1), pivots

    wide, pivots = lax.fori_loop(0, B, step, (wide, jnp.ones((B, 2 * B), F32)))
    return wide[:, :B] * lax.rsqrt(pivots[:, :B])


def chain_kernel(start_ref, weight_ref, gathered, left_ref, image_ref, gram_ref, coef_ref,
                 w, core_out, core_in, z_out, z_in, y_out, y_in, x_out, x_in, acc,
                 ar_out, ar_in, right, raw, own, load_sem, send_sem, recv_sem):
    ny = NYH * NYL
    slab = ny * NX
    row_id = lax.axis_index("row")
    col_id = lax.axis_index("col")
    y_hi, x = row_id // NX, row_id % NX
    z, y_lo, core = col_id // (NYL * NC), (col_id // NC) % NYL, col_id % NC
    y = y_hi * NYL + y_lo

    def device(core, z, y, x):
        return ((y // NYL) * NX + x, (z * NYL + y % NYL) * NC + core)

    def peer(axis, d):
        if axis == "c":
            return device((core + d) % NC, z, y, x)
        if axis == "z":
            return device(core, (z + d) % NZ, y, x)
        if axis == "y":
            return device(core, z, (y + d) % ny, x)
        return device(core, z, y, (x + d) % NX)

    sizes = {"c": NC, "z": NZ, "y": ny, "x": NX}
    peers = [(a, d) for a in "czyx" for d in range(1, sizes[a])]

    def load(p, _):
        pc, pz, py, px = p // (NZ * slab), (p // slab) % NZ, (p // NX) % ny, p % NX
        dr, dc = device(pc, pz, py, px)
        pltpu.make_async_copy(weight_ref.at[dr * (NZ * NYL * NC) + dc], w.at[p, pl.ds(0, ROWS)], load_sem).start()
        return 0

    lax.fori_loop(0, NC * NZ * slab, load, 0)

    barrier = pltpu.get_barrier_semaphore()
    for a, d in peers:
        pl.semaphore_signal(barrier, inc=1, device_id=peer(a, d), device_id_type=MESH)
    pl.semaphore_wait(barrier, len(peers))

    def send_to(target, src, dst, j, phase, d):
        copy = pltpu.make_async_remote_copy(
            src_ref=src, dst_ref=dst, send_sem=send_sem.at[j, phase, d], recv_sem=recv_sem.at[j, phase, d],
            device_id=target, device_id_type=MESH)
        copy.start()
        return copy

    def send(src, dst, j, phase, d, axis):
        return send_to(peer(axis, d), src, dst, j, phase, d)

    def swap(src, dst, j, phase, d):
        return send_to(peer("c", 1), src, dst, j, phase, d)

    w[:, ROWS:, :] = jnp.zeros((NC * NZ * slab, LANES - ROWS, COLS), BF16)

    half = B // NC
    others = {"z": ARZ, "y": ARY, "x": ARX}

    class Reduce:
        def __init__(self, value, j):
            self.j, self.lanes, self.stage = j, value.shape[1], 0
            self.sent = []
            pad = -self.lanes % LANES
            if pad:
                value = jnp.concatenate([value, jnp.zeros((B, pad), F32)], 1)
            self.width = value.shape[1]
            out = ar_out.at[j, 0]
            out[:, : self.width] = value
            mine = pl.ds(pl.multiple_of(core * half, half), half)
            theirs = pl.ds(pl.multiple_of((1 - core) * half, half), half)
            self.mine = mine
            self.pending = [send(ar_out.at[j, 0, theirs, pl.ds(0, self.width)],
                                 ar_in.at[j, 0, 0, pl.ds(0, half), pl.ds(0, self.width)], j, ARC, 1, "c")]
            self.own = out[mine, : self.width]

        def step(self):
            j, width, s = self.j, self.width, self.stage
            total = self.own
            for i, copy in enumerate(self.pending):
                copy.wait_recv()
                if s < 4:
                    total = total + ar_in[j, s, i, 0:half, 0:width]
            self.sent += self.pending
            self.pending = []
            self.stage += 1
            if s < 3:
                axis = "zyx"[s]
                self.own = total
                ar_out[j, s + 1, 0:half, 0:width] = total
                for d in range(1, sizes[axis]):
                    self.pending.append(send(
                        ar_out.at[j, s + 1, pl.ds(0, half), pl.ds(0, width)],
                        ar_in.at[j, s + 1, d - 1, pl.ds(0, half), pl.ds(0, width)], j, others[axis], d, axis))
            elif s == 3:
                ar_in[j, 4, 0, self.mine, 0:width] = total
                there = ar_in.at[j, 4, 0, self.mine, pl.ds(0, width)]
                self.pending.append(send(there, there, j, ARB, 1, "c"))
            else:
                return ar_in[j, 4, 0, :, 0 : self.lanes]
            return None

    def product_slab(low, base):
        def run(put):
            step = min(8, slab)

            def body(g, _):
                block = w[pl.ds(base + g * step, step)].reshape(step * LANES, COLS)
                out = fast(low, block, NT)
                for i in range(step):
                    put(g * step + i, out[:, i * LANES : (i + 1) * LANES])
                return 0

            lax.fori_loop(0, slab // step, body, 0)
        return run

    def base_of(c, zz):
        return (c * NZ + zz) * slab

    pltpu.make_async_copy(weight_ref, w.at[:, pl.ds(0, ROWS)], load_sem).wait()

    raw[...] = start_ref[...]
    coef_ref[...] = jnp.zeros_like(coef_ref)
    z_order = [d % NZ for d in range(1, NZ + 1)]
    for j in range(STEPS):
        done = []
        low = raw[...].astype(BF16)
        right[j * B : (j + 1) * B, :] = raw[...]
        gram = dot(raw[...], right[0 : (j + 1) * B, :], NT)
        if j:
            newest = image_ref[(j - 1) * B : j * B, :]
            gram = jnp.concatenate([gram, dot(newest, image_ref[0 : j * B, :], NT)], 1)
        reduce = Reduce(gram, j)

        core_copies = {}
        for d in z_order:
            def put(i, value, d=d):
                core_out[d, i] = value.astype(BF16)
            product_slab(low, base_of(1 - core, (z + d) % NZ))(put)
            core_copies[d] = swap(core_out.at[d], core_in.at[j, d], j, RSC, d)
        reduce.step()
        z_copies = []
        for d in z_order:
            def put(i, value):
                acc[i] = value
            product_slab(low, base_of(core, (z + d) % NZ))(put)
            core_copies[d].wait_recv()
            if d:
                z_out[d - 1] = (acc[...] + core_in[j, d].astype(F32)).astype(BF16)
                z_copies.append(send(z_out.at[d - 1], z_in.at[j, d - 1], j, RSZ, d, "z"))
            else:
                acc[...] = acc[...] + core_in[j, d].astype(F32)
        done += list(core_copies.values()) + z_copies
        reduce.step()
        reduce.step()
        reduce.step()
        total = reduce.step()
        done += reduce.sent

        cross = total[:, 0 : j * B]
        clean = total[:, j * B : (j + 1) * B]
        if j:
            gram_ref[(j - 1) * B : j * B, 0 : j * B] = total[:, (j + 1) * B : (2 * j + 1) * B]
            clean = clean - dot(cross, cross, NT)
        solve = inverse_factor(clean)
        block = raw[...]
        if j:
            block = block - dot(cross, right[0 : j * B, :])
        right[j * B : (j + 1) * B, :] = dot(solve, block)

        for copy in z_copies:
            copy.wait_recv()
        y_copies = []
        for d in range(1, ny + 1):
            e = d % ny
            at = pl.ds(((y + e) % ny) * NX, NX)
            value = acc[at]
            for i in range(NZ - 1):
                value = value + z_in[j, i, at].astype(F32)
            if e:
                y_out[e - 1] = value
                y_copies.append(send(y_out.at[e - 1], y_in.at[j, e - 1], j, RSY, e, "y"))
            else:
                acc[at] = value
        for copy in y_copies:
            copy.wait_recv()
        x_copies = []
        for d in range(1, NX + 1):
            e = d % NX
            at = (x + e) % NX
            value = acc[y * NX + at]
            for i in range(ny - 1):
                value = value + y_in[j, i, at]
            if e:
                x_out[e - 1] = value
                x_copies.append(send(x_out.at[e - 1], x_in.at[j, e - 1], j, RSX, e, "x"))
            else:
                mine = value
        for i, copy in enumerate(x_copies):
            copy.wait_recv()
            mine = mine + x_in[j, i]
        done += y_copies + x_copies
        if j:
            mine = mine - dot(cross, own[0 : j * B, :])
        mine = dot(solve, mine)
        own[j * B : (j + 1) * B, :] = mine

        place = ((core * NZ + z) * ny + y) * NX + x
        gathered[j, place] = mine.astype(BF16)

        def spread(axis, phase, at, n):
            piece = gathered.at[j, pl.ds(at, n)]
            return [send(piece, piece, j, phase, d, axis) for d in range(1, sizes[axis])]

        for axis, phase, at, n in (("x", AGX, place, 1), ("y", AGY, place - x, NX)):
            copies = spread(axis, phase, at, n)
            for copy in copies:
                copy.wait_recv()
            done += copies
        copies = spread("z", AGZ, base_of(core, z), slab)
        done += copies

        def back_slab(carry, base):
            step = min(8, slab)

            def body(g, carry):
                image, gram = carry
                at = pl.ds(base + g * step, step)
                pieces = [gathered[j, base + g * step + i] for i in range(step)]
                newest = jnp.concatenate(pieces, 1)
                image = image + fast(newest, w[at].reshape(step * LANES, COLS))
                grams = []
                for k in range(j + 1):
                    piece = newest if k == j else jnp.concatenate(
                        [gathered[k, base + g * step + i] for i in range(step)], 1)
                    grams.append(gram[k] + fast(newest, piece, NT))
                return image, tuple(grams)

            return lax.fori_loop(0, slab // step, body, carry)

        def handed(d):
            piece = gathered.at[j, pl.ds(base_of(core, (z + d) % NZ), slab)]
            return swap(piece, piece, j, AGC, d)

        carry = (jnp.zeros((B, COLS), F32), tuple(jnp.zeros((B, B), F32) for _ in range(j + 1)))
        handed_on = {0: handed(0)}
        carry = back_slab(carry, base_of(core, z))
        for d in range(1, NZ):
            copies[d - 1].wait_recv()
            handed_on[(NZ - d) % NZ] = handed((NZ - d) % NZ)
            carry = back_slab(carry, base_of(core, (z + NZ - d) % NZ))
        for d in [0] + [(NZ - d) % NZ for d in range(1, NZ)]:
            handed_on[d].wait_recv()
            carry = back_slab(carry, base_of(1 - core, (z + d) % NZ))
        done += list(handed_on.values())
        image, grams = carry

        clean = grams[j]
        if j:
            table = coef_ref[0 : j * B, 0 : j * B]
            cross = dot(jnp.concatenate(grams[:j], 1), table, NT)
            clean = clean - dot(cross, cross, NT)
        solve = inverse_factor(clean)
        if j:
            image = image - dot(cross, image_ref[0 : j * B, :])
        image = dot(solve, image)
        image_ref[j * B : (j + 1) * B, :] = image
        if j + 1 < STEPS:
            raw[...] = image - dot(dot(solve, clean), right[j * B : (j + 1) * B, :])
        left = mine
        if j:
            left = left - dot(cross, left_ref[0 : j * B, :])
            coef_ref[j * B : (j + 1) * B, 0 : j * B] = -dot(solve, dot(cross, table))
        left_ref[j * B : (j + 1) * B, :] = dot(solve, left)
        coef_ref[j * B : (j + 1) * B, j * B : (j + 1) * B] = solve
        for copy in done:
            copy.wait_send()

    reduce = Reduce(dot(image_ref[(STEPS - 1) * B :, :], image_ref[...], NT), STEPS)
    total = None
    while total is None:
        total = reduce.step()
    gram_ref[(STEPS - 1) * B :, :] = total
    for copy in reduce.sent:
        copy.wait_send()


def chain(start_t, blocks):
    ny = NYH * NYL
    slab = ny * NX
    n = NC * NZ * slab
    vmem = pl.BlockSpec(memory_space=pltpu.VMEM)
    s = STEPS * B
    return pl.pallas_call(
        chain_kernel,
        out_shape=(
            jax.ShapeDtypeStruct((STEPS, n, B, LANES), BF16),
            jax.ShapeDtypeStruct((s, LANES), F32),
            jax.ShapeDtypeStruct((s, COLS), F32),
            jax.ShapeDtypeStruct((s, s), F32),
            jax.ShapeDtypeStruct((s, s), F32),
        ),
        in_specs=[vmem, pl.BlockSpec(memory_space=pl.ANY)],
        out_specs=[vmem] * 5,
        scratch_shapes=[
            pltpu.VMEM((n, LANES, COLS), BF16),
            pltpu.VMEM((NZ, slab, B, LANES), BF16),
            pltpu.VMEM((STEPS, NZ, slab, B, LANES), BF16),
            pltpu.VMEM((NZ - 1, slab, B, LANES), BF16),
            pltpu.VMEM((STEPS, NZ - 1, slab, B, LANES), BF16),
            pltpu.VMEM((ny - 1, NX, B, LANES), F32),
            pltpu.VMEM((STEPS, ny - 1, NX, B, LANES), F32),
            pltpu.VMEM((NX - 1, B, LANES), F32),
            pltpu.VMEM((STEPS, NX - 1, B, LANES), F32),
            pltpu.VMEM((slab, B, LANES), F32),
            pltpu.VMEM((STEPS + 1, 4, B, 3 * LANES), F32),
            pltpu.VMEM((STEPS + 1, 5, 3, B, 3 * LANES), F32),
            pltpu.VMEM((s, COLS), F32),
            pltpu.VMEM((B, COLS), F32),
            pltpu.VMEM((s, LANES), F32),
            pltpu.SemaphoreType.DMA,
            pltpu.SemaphoreType.DMA((STEPS + 1, 13, 4)),
            pltpu.SemaphoreType.DMA((STEPS + 1, 13, 4)),
        ],
        compiler_params=pltpu.CompilerParams(
            collective_id=0, has_side_effects=True, vmem_limit_bytes=60 * 1024 * 1024),
    )(start_t, blocks)


def sweep_kernel(gram_ref, coef_ref, basis_ref, high_ref, low_ref):
    g = [[None] * STEPS for _ in range(STEPS)]
    for i in range(STEPS):
        for k in range(i + 1):
            g[i][k] = gram_ref[i * B : (i + 1) * B, k * B : (k + 1) * B]
            if k < i:
                g[k][i] = g[i][k].T
    whole = jnp.concatenate([jnp.concatenate(r, 1) for r in g], 0)

    def orth(grown):
        top, bottom = grown[:B], grown[B:]
        one = inverse_factor(dot(top, top, NT))
        first = dot(one, top)
        cross = dot(bottom, first, NT)
        clean = bottom - dot(cross, first)
        two = inverse_factor(dot(clean, clean, NT))
        return jnp.concatenate([first, dot(two, clean)], 0)

    basis = orth(whole[:RANK])
    basis = lax.fori_loop(1, SWEEPS, lambda _, basis: orth(dot(basis, whole)), basis)
    basis_ref[...] = basis
    mixed = dot(basis, coef_ref[...])
    high = mixed.astype(BF16)
    high_ref[...] = high
    low_ref[...] = (mixed - high.astype(F32)).astype(BF16)


def sweeps(gram, coef):
    s = STEPS * B
    return pl.pallas_call(
        sweep_kernel,
        out_shape=(
            jax.ShapeDtypeStruct((RANK, s), F32),
            jax.ShapeDtypeStruct((RANK, s), BF16),
            jax.ShapeDtypeStruct((RANK, s), BF16),
        ),
    )(gram, coef)


PER = 8


def residual_kernel(gathered, high, low, right, weight, out):
    ny = NYH * NYL
    first = pl.program_id(0) * PER
    pieces = []
    for i in range(PER):
        at = first + i
        r, c = at // (NZ * NYL * NC), at % (NZ * NYL * NC)
        place = (((c % NC) * NZ + c // (NYL * NC)) * ny + (r // NX) * NYL + (c // NC) % NYL) * NX + r % NX
        pieces.append(jnp.concatenate([gathered[k, place] for k in range(STEPS)], 0))
    stacked = jnp.concatenate(pieces, 1)
    left = (fast(high[...], stacked) + fast(low[...], stacked)).astype(BF16).T
    update = fast(left, right[...], NT)
    for i in range(PER):
        out[i * ROWS : (i + 1) * ROWS, :] = (
            weight[i].astype(F32) - update[i * LANES : i * LANES + ROWS, :]).astype(BF16)


def residual(gathered, high, low, right, blocks):
    n = blocks.shape[0]
    whole = lambda a: pl.BlockSpec(a.shape, lambda i: (0,) * a.ndim)
    return pl.pallas_call(
        residual_kernel,
        grid=(n // PER,),
        out_shape=jax.ShapeDtypeStruct((n * ROWS, COLS), BF16),
        in_specs=[whole(gathered), whole(high), whole(low), whole(right),
                  pl.BlockSpec((PER, ROWS, COLS), lambda i: (i, 0, 0))],
        out_specs=pl.BlockSpec((PER * ROWS, COLS), lambda i: (i, 0)),
        compiler_params=pltpu.CompilerParams(vmem_limit_bytes=48 * 1024 * 1024),
    )(gathered, high, low, right, blocks)


def shards(weight, start):
    rows, cols = NYH * NX, NZ * NYL * NC
    n = rows * cols
    parts = weight.reshape(ROWS, cols, rows, COLS).transpose(2, 1, 0, 3).reshape(n, ROWS, COLS)
    blocks = lax.all_to_all(parts, ("row", "col"), split_axis=0, concat_axis=0, tiled=True)
    gathered, left, images, gram, coef = chain(start.T, blocks)
    basis, high, low = sweeps(gram, coef)
    adapter_left = lax.dot_general(left[:, :ROWS], basis, (((0,), (1,)), ((), ())), precision=HIGHEST,
                                   preferred_element_type=F32)
    adapter_right = lax.dot_general(images, basis, (((0,), (1,)), ((), ())), precision=HIGHEST,
                                    preferred_element_type=F32)
    out = residual(gathered, high, low, adapter_right.astype(BF16), blocks)
    return (adapter_left, adapter_right, out)


def solution(mesh):
    return jax.shard_map(
        shards,
        mesh=mesh,
        in_specs=(P(("row", "col"), None), P(("col", "row"), None)),
        out_specs=(P(("row", "col"), None), P(("col", "row"), None), P(None, ("col", "row"))),
        check_vma=False,
    )
```

time: 1970 us -> 635 us (0.32)
  blocking collectives: 1100 us -> 171 us
  waiting for transfers between devices: 538 us -> 0 us
  Pallas kernels: 0 us -> 393 us
  other arithmetic: 164 us -> 0 us
  matrix products: 74.3 us -> 4.66 us
    psum x10 -> x0, blocking collectives: 774 us -> none  [sum_everywhere(): return lax.psum(values, ('row', 'col'))]
    pallas_call x0 -> x3, Pallas kernels: none -> 393 us  [the longest x1 277 us: chain(): pl.pallas_call(chain_kernel, out_shape=(jax.ShapeDtypeStruct((STEPS, n, B...]
    unnamed x13 -> x0, waiting for transfers between devices: 391 us -> none
    all_gather x8 -> x0, blocking collectives: 195 us -> none  [the longest x3 87.3 us: shards(): whole_right = lax.all_gather(low_right, 'row', axis=0, tiled=True)]
    another operation x50 -> x0, other arithmetic: 164 us -> none  [the longest x30 88.9 us: finish(): factor = jnp.linalg.cholesky(gram_matrix)]
    psum x1 -> x0, waiting for transfers between devices: 146 us -> none  [sum_everywhere(): return lax.psum(values, ('row', 'col'))]
    dot_general x32 -> x2, matrix products: 71.5 us -> 4.66 us  [the longest x1 2.68 us: shards(): lax.dot_general(images, basis, (((0,), (1,)), ((), ())), precision=HIGHES...]
    all_to_all x1, blocking collectives: 132 us -> 171 us  [shards(): lax.all_to_all(parts, ('row', 'col'), split_axis=0, concat_axis=0, tiled=...]
  transfers between devices with their start and end apart: 8 -> 0, of which waited for: 7 -> 0; matrix products, arithmetic and copies ran while one was open for 1% -> 0% of each run, Pallas kernels for 0% -> 0%
where the time goes in v1:
time: 635 us; the launch traced here: 633 us
  Pallas kernels  393 us (62%)
  blocking collectives  171 us (27%)
  local copies, waits for them, and re-layouts  63 us (10%)
    pallas_call x1, Pallas kernels, chain(): pl.pallas_call(chain_kernel, out_shape=(jax.ShapeDtypeStruct((STEPS, n, B...  277 us
    all_to_all x1, blocking collectives, shards(): lax.all_to_all(parts, ('row', 'col'), split_axis=0, concat_axis=0, tiled=...  171 us
    pallas_call x1, Pallas kernels, sweeps(): pl.pallas_call(sweep_kernel, out_shape=(jax.ShapeDtypeStruct((RANK, s), F...  94.3 us
    unnamed x6, local copies, waits for them, and re-layouts  36 us
    pallas_call x1, Pallas kernels, residual(): pl.pallas_call(residual_kernel, grid=(n // PER,), out_shape=jax.ShapeDtyp...  21.9 us
    all_to_all x1, local copies, waits for them, and re-layouts, shards(): lax.all_to_all(parts, ('row', 'col'), split_axis=0, concat_axis=0, tiled=...  19.3 us

profile of v1, /device:TPU:1, one launch (start us, length us, event | category | flops | bytes accessed | tf_op | source)
XLA Modules:
  0.0 633.0 jit_solution(18024500083610480552)
XLA Ops:
  0.6 16.9 %copy.14 = bf16[112,53248]{0,1:T(8,128)(2,1)} copy(bf16[112,53248]{1,0:T(8,128)(2,1)} %param.2) | data formatting | bytes 23855104 | tf_op args[0]
  17.5 7.7 %copy.15 = bf16[8,16,112,416]{2,3,1,0:T(8,128)(2,1)S(1)} copy(bf16[8,16,112,416]{2,3,0,1:T(8,128)(2,1)} %bitcast.8) | data formatting | bytes 23855104 | tf_op jit(solution)/shard_map/transpose | solution.py:460
  25.2 171.4 %all_to_all.5 = bf16[128,112,416]{1,2,0:T(8,128)(2,1)} all-to-all(bf16[128,112,416]{1,2,0:T(8,128)(2,1)S(1)} %bitcast.9), channel_id=1, replica_groups=mesh['row'=8,'col'=16] {'row','col'}, dimensions={0} | all-to-all | bytes 23855104 | tf_op jit(solution)/shard_map/all_to_all | solution.py:461
  196.6 19.3 %copy.16.weight_ref.weight = bf16[128,112,416]{2,1,0:T(8,128)(2,1)} copy(bf16[128,112,416]{1,2,0:T(8,128)(2,1)} %all_to_all.5) | data formatting | bytes 23855104 | tf_op jit(solution)/shard_map/all_to_all | solution.py:461
  215.9 277.1 %shard_map.49 = (bf16[3,128,64,128]{3,2,1,0:T(8,128)(2,1)}, f32[192,128]{1,0:T(8,128)}, f32[192,416]{1,0:T(8,128)}, f32[192,192]{1,0:T(8,128)}, f32[192,192]{1,0:T(8,128)}) custom-call(f32[64,416]{1,0:T(8,128)} %bitcast.10, bf16[128,112,416]{2,1,0:T(8,128)(2,1)} %copy.16.weight_ref.weight), custom_call_target="tpu_custom_call" | custom-call | tf_op jit(solution)/shard_map/pallas_call | solution.py:348
  493.0 94.3 %shard_map.50 = (f32[128,192]{1,0:T(8,128)}, bf16[128,192]{1,0:T(8,128)(2,1)}, bf16[128,192]{1,0:T(8,128)(2,1)}) custom-call(f32[192,192]{1,0:T(8,128)} %get-tuple-element.12.gram_ref, f32[192,192]{1,0:T(8,128)} %get-tuple-element.13.coef_ref), custom_call_target="tpu_custom_call" | custom-call | tf_op jit(solution)/shard_map/pallas_call | solution.py:413
  587.2 2.7 fusion.2
  589.9 2.0 fusion
  591.9 0.0 copy-start
  591.9 0.8 copy-done
  592.7 0.0 copy-start.1
  592.7 0.8 copy-done.1
  593.6 21.9 %shard_map.51 = bf16[14336,416]{1,0:T(8,128)(2,1)} custom-call(bf16[3,128,64,128]{3,2,1,0:T(8,128)(2,1)} %get-tuple-element.16.gathered, bf16[128,192]{1,0:T(8,128)(2,1)S(1)} %copy-done, bf16[128,192]{1,0:T(8,128)(2,1)S(1)} %copy-done.1, bf16[416,128]{1,0:T(8,128)(2,1)S(1)} %get-tuple-element.31.right, bf16[128,112,416]{2,1,0:T(8,128)(2,1)} %copy.16.weight_ref.weight), custom_call_target="tpu_custom_call" | custom-call | tf_op jit(solution)/shard_map/pallas_call | solution.py:446
  615.5 17.5 %copy.18 = bf16[14336,416]{0,1:T(8,128)(2,1)} copy(bf16[14336,416]{1,0:T(8,128)(2,1)} %shard_map.51) | data formatting | bytes 23855104
Async XLA Ops:
  591.9 0.8 copy-start
  592.7 0.8 copy-start.1

commit v2 on v1

--- a/solution.py
+++ b/solution.py
@@ -35,23 +35,30 @@
 
 
 def inverse_factor(gram):
-    sub = lax.broadcasted_iota(jnp.int32, (B, 2 * B), 0)
-    lane = lax.broadcasted_iota(jnp.int32, (B, 2 * B), 1)
+    sub = lax.broadcasted_iota(jnp.int32, (8, LANES), 0)
+    lane = lax.broadcasted_iota(jnp.int32, (8, LANES), 1)
     wide = jnp.concatenate([gram, jnp.zeros_like(gram)], 1)
-    wide = jnp.where(lane == sub + B, 1.0, wide)
-
-    def step(k, carry):
-        wide, pivots = carry
-        row = jnp.sum(jnp.where(sub == k, wide, 0.0), axis=0, keepdims=True)
-        pivot = row[:, 0:1]
-        scaled = row * (1.0 / pivot)
-        column = jnp.where(sub[:, 0:1] > k, wide[:, 0:1], 0.0)
-        wide = wide - column * scaled
-        pivots = jnp.where(sub == k, pivot, pivots)
-        return pltpu.roll(wide, 2 * B - 1, 1), pivots
-
-    wide, pivots = lax.fori_loop(0, B, step, (wide, jnp.ones((B, 2 * B), F32)))
-    return wide[:, :B] * lax.rsqrt(pivots[:, :B])
+    n = B // 8
+    rows = [jnp.where(lane == sub + (B + 8 * q), 1.0, wide[8 * q : 8 * q + 8]) for q in range(n)]
+    for p in range(n):
+        columns = {q: [jnp.broadcast_to(rows[q][:, 8 * p + k : 8 * p + k + 1], (8, LANES)) for k in range(8)]
+                   for q in range(p, n)}
+        scale = jnp.ones((8, LANES), F32)
+        for k in range(8):
+            pivot = columns[p][k][k : k + 1]
+            inverse = 1.0 / pivot
+            scale = jnp.where(sub == k, lax.rsqrt(pivot), scale)
+            row = rows[p][k : k + 1] * inverse
+            ahead = {i: columns[p][i][k : k + 1] * inverse for i in range(k + 1, 8)}
+            for q in range(p, n):
+                factor = columns[q][k]
+                if q == p:
+                    factor = jnp.where(sub > k, factor, 0.0)
+                rows[q] = rows[q] - factor * row
+                for i in range(k + 1, 8):
+                    columns[q][i] = columns[q][i] - factor * ahead[i]
+        rows[p] = rows[p] * scale
+    return jnp.concatenate(rows, 0)[:, B:]
 
 
 def chain_kernel(start_ref, weight_ref, gathered, left_ref, image_ref, gram_ref, coef_ref,
@@ -83,7 +90,7 @@
     def load(p, _):
         pc, pz, py, px = p // (NZ * slab), (p // slab) % NZ, (p // NX) % ny, p % NX
         dr, dc = device(pc, pz, py, px)
-        pltpu.make_async_copy(weight_ref.at[dr * (NZ * NYL * NC) + dc], w.at[p, pl.ds(0, ROWS)], load_sem).start()
+        pltpu.make_async_copy(weight_ref.at[dr * (NZ * NYL * NC) + dc], w.at[p], load_sem).start()
         return 0
 
     lax.fori_loop(0, NC * NZ * slab, load, 0)
@@ -105,8 +112,6 @@
 
     def swap(src, dst, j, phase, d):
         return send_to(peer("c", 1), src, dst, j, phase, d)
-
-    w[:, ROWS:, :] = jnp.zeros((NC * NZ * slab, LANES - ROWS, COLS), BF16)
 
     half = B // NC
     others = {"z": ARZ, "y": ARY, "x": ARX}
@@ -159,8 +164,8 @@
             step = min(8, slab)
 
             def body(g, _):
-                block = w[pl.ds(base + g * step, step)].reshape(step * LANES, COLS)
-                out = fast(low, block, NT)
+                block = jnp.concatenate([w[base + g * step + i] for i in range(step)], 1)
+                out = fast(low, block)
                 for i in range(step):
                     put(g * step + i, out[:, i * LANES : (i + 1) * LANES])
                 return 0
@@ -171,7 +176,7 @@
     def base_of(c, zz):
         return (c * NZ + zz) * slab
 
-    pltpu.make_async_copy(weight_ref, w.at[:, pl.ds(0, ROWS)], load_sem).wait()
+    pltpu.make_async_copy(weight_ref, w, load_sem).wait()
 
     raw[...] = start_ref[...]
     coef_ref[...] = jnp.zeros_like(coef_ref)
@@ -279,10 +284,10 @@
 
             def body(g, carry):
                 image, gram = carry
-                at = pl.ds(base + g * step, step)
                 pieces = [gathered[j, base + g * step + i] for i in range(step)]
                 newest = jnp.concatenate(pieces, 1)
-                image = image + fast(newest, w[at].reshape(step * LANES, COLS))
+                block = jnp.concatenate([w[base + g * step + i] for i in range(step)], 1)
+                image = image + fast(newest, block, NT)
                 grams = []
                 for k in range(j + 1):
                     piece = newest if k == j else jnp.concatenate(
@@ -357,7 +362,7 @@
         in_specs=[vmem, pl.BlockSpec(memory_space=pl.ANY)],
         out_specs=[vmem] * 5,
         scratch_shapes=[
-            pltpu.VMEM((n, LANES, COLS), BF16),
+            pltpu.VMEM((n, COLS, LANES), BF16),
             pltpu.VMEM((NZ, slab, B, LANES), BF16),
             pltpu.VMEM((STEPS, NZ, slab, B, LANES), BF16),
             pltpu.VMEM((NZ - 1, slab, B, LANES), BF16),
@@ -434,10 +439,18 @@
         pieces.append(jnp.concatenate([gathered[k, place] for k in range(STEPS)], 0))
     stacked = jnp.concatenate(pieces, 1)
     left = (fast(high[...], stacked) + fast(low[...], stacked)).astype(BF16).T
-    update = fast(left, right[...], NT)
-    for i in range(PER):
-        out[i * ROWS : (i + 1) * ROWS, :] = (
-            weight[i].astype(F32) - update[i * LANES : i * LANES + ROWS, :]).astype(BF16)
+    left = jnp.concatenate([left[i * LANES : i * LANES + ROWS] for i in range(PER)], 0)
+    update = fast(right[...], left, NT)
+    lane = lax.broadcasted_iota(jnp.int32, (COLS, LANES), 1)
+    gap = LANES - ROWS
+    for t in range(PER * ROWS // LANES):
+        block = weight[t].astype(F32)
+        if t:
+            block = pltpu.roll(block, LANES - gap * t, 1)
+        after = pltpu.roll(weight[t + 1].astype(F32), ROWS - gap * t, 1)
+        block = jnp.where(lane < ROWS - gap * t, block, after)
+        at = slice(t * LANES, (t + 1) * LANES)
+        out[:, at] = (block - update[:, at]).astype(BF16)
 
 
 def residual(gathered, high, low, right, blocks):
@@ -446,10 +459,10 @@
     return pl.pallas_call(
         residual_kernel,
         grid=(n // PER,),
-        out_shape=jax.ShapeDtypeStruct((n * ROWS, COLS), BF16),
+        out_shape=jax.ShapeDtypeStruct((COLS, n * ROWS), BF16),
         in_specs=[whole(gathered), whole(high), whole(low), whole(right),
-                  pl.BlockSpec((PER, ROWS, COLS), lambda i: (i, 0, 0))],
-        out_specs=pl.BlockSpec((PER * ROWS, COLS), lambda i: (i, 0)),
+                  pl.BlockSpec((PER, COLS, LANES), lambda i: (i, 0, 0))],
+        out_specs=pl.BlockSpec((COLS, PER * ROWS), lambda i: (0, i)),
         compiler_params=pltpu.CompilerParams(vmem_limit_bytes=48 * 1024 * 1024),
     )(gathered, high, low, right, blocks)
 
@@ -457,7 +470,8 @@
 def shards(weight, start):
     rows, cols = NYH * NX, NZ * NYL * NC
     n = rows * cols
-    parts = weight.reshape(ROWS, cols, rows, COLS).transpose(2, 1, 0, 3).reshape(n, ROWS, COLS)
+    padded = jnp.pad(weight, ((0, LANES - ROWS), (0, 0)))
+    parts = padded.T.reshape(cols, rows, COLS, LANES).transpose(1, 0, 2, 3).reshape(n, COLS, LANES)
     blocks = lax.all_to_all(parts, ("row", "col"), split_axis=0, concat_axis=0, tiled=True)
     gathered, left, images, gram, coef = chain(start.T, blocks)
     basis, high, low = sweeps(gram, coef)
@@ -466,7 +480,7 @@
     adapter_right = lax.dot_general(images, basis, (((0,), (1,)), ((), ())), precision=HIGHEST,
                                     preferred_element_type=F32)
     out = residual(gathered, high, low, adapter_right.astype(BF16), blocks)
-    return (adapter_left, adapter_right, out)
+    return (adapter_left, adapter_right, out.T)
 
 
 def solution(mesh):

time: 635 us -> 468 us (0.74)
  Pallas kernels: 393 us -> 263 us
  local copies, waits for them, and re-layouts: 63 us -> 26.7 us
    pallas_call x1, Pallas kernels: 94.3 us -> 20.4 us  [sweeps(): pl.pallas_call(sweep_kernel, out_shape=(jax.ShapeDtypeStruct((RANK, s), F...]
    pallas_call x1, Pallas kernels: 277 us -> 221 us  [chain(): pl.pallas_call(chain_kernel, out_shape=(jax.ShapeDtypeStruct((STEPS, n, B...]
    all_to_all x1 -> x0, local copies, waits for them, and re-layouts: 19.3 us -> none  [shards(): lax.all_to_all(parts, ('row', 'col'), split_axis=0, concat_axis=0, tiled=...]
    unnamed x6 -> x5, local copies, waits for them, and re-layouts: 36 us -> 18.6 us
where the time goes in v2:
time: 468 us; the launch traced here: 466 us
  Pallas kernels  263 us (56%)
  blocking collectives  171 us (37%)
  local copies, waits for them, and re-layouts  26.7 us (6%)
    pallas_call x1, Pallas kernels, chain(): pl.pallas_call(chain_kernel, out_shape=(jax.ShapeDtypeStruct((STEPS, n, B...  221 us
    all_to_all x1, blocking collectives, shards(): lax.all_to_all(parts, ('row', 'col'), split_axis=0, concat_axis=0, tiled=...  171 us
    pallas_call x1, Pallas kernels, residual(): pl.pallas_call(residual_kernel, grid=(n // PER,), out_shape=jax.ShapeDtyp...  21.6 us
    pallas_call x1, Pallas kernels, sweeps(): pl.pallas_call(sweep_kernel, out_shape=(jax.ShapeDtypeStruct((RANK, s), F...  20.4 us
    unnamed x5, local copies, waits for them, and re-layouts  18.6 us

profile of v2, /device:TPU:1, one launch (start us, length us, event | category | flops | bytes accessed | tf_op | source)
XLA Modules:
  0.0 466.5 jit_solution(10645515940432827644)
XLA Ops:
  0.6 16.9 %copy.6 = bf16[112,53248]{0,1:T(8,128)(2,1)} copy(bf16[112,53248]{1,0:T(8,128)(2,1)} %param.2) | data formatting | bytes 23855104 | tf_op args[0]
  17.5 6.2 %pad.4 = bf16[128,53248]{0,1:T(8,128)(2,1)S(1)} pad(bf16[112,53248]{0,1:T(8,128)(2,1)} %copy.6, bf16[]{:T(256)} %constant.2.clone.1), padding=0_16x0_0 | pad | bytes 25559042 | tf_op jit(solution)/shard_map/jit(_pad)/pad | solution.py:473
  23.7 1.9 copy.7
  25.6 171.4 %all_to_all.5.weight_ref.weight = bf16[128,416,128]{2,1,0:T(8,128)(2,1)} all-to-all(bf16[128,416,128]{2,1,0:T(8,128)(2,1)S(1)} %bitcast.12), channel_id=1, replica_groups=mesh['row'=8,'col'=16] {'row','col'}, dimensions={0} | all-to-all | bytes 27262976 | tf_op jit(solution)/shard_map/all_to_all | solution.py:475
  197.0 221.1 %shard_map.49 = (bf16[3,128,64,128]{3,2,1,0:T(8,128)(2,1)}, f32[192,128]{1,0:T(8,128)}, f32[192,416]{1,0:T(8,128)}, f32[192,192]{1,0:T(8,128)}, f32[192,192]{1,0:T(8,128)}) custom-call(f32[64,416]{1,0:T(8,128)} %bitcast.14, bf16[128,416,128]{2,1,0:T(8,128)(2,1)} %all_to_all.5.weight_ref.weight), custom_call_target="tpu_custom_call" | custom-call | tf_op jit(solution)/shard_map/pallas_call | solution.py:353
  418.1 20.4 %shard_map.50 = (f32[128,192]{1,0:T(8,128)}, bf16[128,192]{1,0:T(8,128)(2,1)}, bf16[128,192]{1,0:T(8,128)(2,1)}) custom-call(f32[192,192]{1,0:T(8,128)} %get-tuple-element.12.gram_ref, f32[192,192]{1,0:T(8,128)} %get-tuple-element.13.coef_ref), custom_call_target="tpu_custom_call" | custom-call | tf_op jit(solution)/shard_map/pallas_call | solution.py:418
  438.5 2.7 fusion.2
  441.2 2.0 fusion
  443.2 0.0 copy-start
  443.2 0.8 copy-done
  444.0 0.0 copy-start.1
  444.0 0.8 copy-done.1
  444.8 21.6 %shard_map.51 = bf16[416,14336]{1,0:T(8,128)(2,1)} custom-call(bf16[3,128,64,128]{3,2,1,0:T(8,128)(2,1)} %get-tuple-element.16.gathered, bf16[128,192]{1,0:T(8,128)(2,1)S(1)} %copy-done, bf16[128,192]{1,0:T(8,128)(2,1)S(1)} %copy-done.1, bf16[416,128]{1,0:T(8,128)(2,1)S(1)} %get-tuple-element.19.right, bf16[128,416,128]{2,1,0:T(8,128)(2,1)} %all_to_all.5.weight_ref.weight), custom_call_target="tpu_custom_call" | custom-call | tf_op jit(solution)/shard_map/pallas_call | solution.py:459
Async XLA Ops:
  443.2 0.8 copy-start
  444.0 0.8 copy-start.1

commit v3 on v2

--- a/solution.py
+++ b/solution.py
@@ -23,7 +23,9 @@
 NT = (((1,), (1,)), ((), ()))
 NN = (((1,), (0,)), ((), ()))
 
-RSC, RSZ, RSY, RSX, AGX, AGY, AGZ, AGC, ARC, ARZ, ARY, ARX, ARB = range(13)
+STREAMS = ((0, 32, "zyx"), (32, 48, "yxz"), (48, 64, "xzy"))
+RSC, RS, AG, AGC, ARC, ARZ, ARY, ARX, ARB = 0, 1, 10, 19, 20, 21, 22, 23, 24
+EXCHANGES = 25
 
 
 def dot(left, right, dims=NN):
@@ -61,19 +63,25 @@
     return jnp.concatenate(rows, 0)[:, B:]
 
 
-def chain_kernel(start_ref, weight_ref, gathered, left_ref, image_ref, gram_ref, coef_ref,
-                 w, core_out, core_in, z_out, z_in, y_out, y_in, x_out, x_in, acc,
-                 ar_out, ar_in, right, raw, own, load_sem, send_sem, recv_sem):
+def chain_kernel(start_ref, weight_ref, gathered, left_ref, image_ref, gram_ref, coef_ref, blocks_ref,
+                 w, strip, staged, core_out, core_in, out1, in1, out2, in2, out3, in3, acc,
+                 ar_out, ar_in, right, raw, own, strip_sem, keep_sem, put_sem, get_sem, send_sem, recv_sem):
     ny = NYH * NYL
     slab = ny * NX
+    n = NC * NZ * slab
     row_id = lax.axis_index("row")
     col_id = lax.axis_index("col")
     y_hi, x = row_id // NX, row_id % NX
     z, y_lo, core = col_id // (NYL * NC), (col_id // NC) % NYL, col_id % NC
     y = y_hi * NYL + y_lo
+    here = {"z": z, "y": y, "x": x}
+    sizes = {"c": NC, "z": NZ, "y": ny, "x": NX}
 
     def device(core, z, y, x):
         return ((y // NYL) * NX + x, (z * NYL + y % NYL) * NC + core)
+
+    def spot(core, z, y, x):
+        return ((core * NZ + z) * ny + y) * NX + x
 
     def peer(axis, d):
         if axis == "c":
@@ -84,21 +92,78 @@
             return device(core, z, (y + d) % ny, x)
         return device(core, z, y, (x + d) % NX)
 
-    sizes = {"c": NC, "z": NZ, "y": ny, "x": NX}
-    peers = [(a, d) for a in "czyx" for d in range(1, sizes[a])]
-
-    def load(p, _):
-        pc, pz, py, px = p // (NZ * slab), (p // slab) % NZ, (p // NX) % ny, p % NX
-        dr, dc = device(pc, pz, py, px)
-        pltpu.make_async_copy(weight_ref.at[dr * (NZ * NYL * NC) + dc], w.at[p], load_sem).start()
+    place = spot(core, z, y, x)
+
+    groups = n // NX
+
+    def offset(i):
+        step, g = i // ny, i % ny
+        return step // NZ, (g + step % NZ) % NZ, g
+
+    def strip_copy(i):
+        dc, dz, dy = offset(i)
+        dr, dl = device((core + dc) % NC, (z + dz) % NZ, (y + dy) % ny, 0)
+        block = dl * (NYH * NX) + dr
+        return pltpu.make_async_copy(
+            weight_ref.at[:, pl.ds(pl.multiple_of(block * COLS, LANES), NX * COLS)], strip.at[i % 2],
+            strip_sem.at[i % 2])
+
+    def block_copy(i, dx):
+        dc, dz, dy = offset(i)
+        tx = (x + dx) % NX
+        return pltpu.make_async_remote_copy(
+            src_ref=staged.at[i, tx], dst_ref=w.at[place], send_sem=put_sem.at[i, dx], recv_sem=get_sem.at[i, dx],
+            device_id=device((core + dc) % NC, (z + dz) % NZ, (y + dy) % ny, tx), device_id_type=MESH)
+
+    strip_copy(0).start()
+    barrier = pltpu.get_barrier_semaphore()
+
+    def greet(d, _):
+        to = (place + d) % n
+        target = device(to // (NZ * slab), (to // slab) % NZ, (to // NX) % ny, to % NX)
+        pl.semaphore_signal(barrier, inc=1, device_id=target, device_id_type=MESH)
         return 0
 
-    lax.fori_loop(0, NC * NZ * slab, load, 0)
-
-    barrier = pltpu.get_barrier_semaphore()
-    for a, d in peers:
-        pl.semaphore_signal(barrier, inc=1, device_id=peer(a, d), device_id_type=MESH)
-    pl.semaphore_wait(barrier, len(peers))
+    lax.fori_loop(1, n, greet, 0)
+
+    def stage(i):
+        strip_copy(i).wait()
+
+        @pl.when(i < groups - 1)
+        def _():
+            strip_copy(i + 1).start()
+
+        value = strip[i % 2]
+        value = jnp.concatenate([value, jnp.zeros((LANES - ROWS, NX * COLS), BF16)], 0).T
+        staged[i] = value.reshape(NX, COLS, LANES)
+
+    def scatter(step, _):
+        def each(g, _):
+            stage(step * ny + g)
+            return 0
+
+        lax.fori_loop(0, ny, each, 0)
+
+        @pl.when(step == 0)
+        def _():
+            pl.semaphore_wait(barrier, n - 1)
+            pltpu.make_async_copy(staged.at[0, x], w.at[place], keep_sem).start()
+
+        def rotate(a, _):
+            for dx in range(NX):
+                i = step * ny + (dx + a) % ny
+                if dx == 0:
+                    @pl.when(i != 0)
+                    def _():
+                        block_copy(i, dx).start()
+                else:
+                    block_copy(i, dx).start()
+            return 0
+
+        lax.fori_loop(0, ny, rotate, 0)
+        return 0
+
+    lax.fori_loop(0, groups // ny, scatter, 0)
 
     def send_to(target, src, dst, j, phase, d):
         copy = pltpu.make_async_remote_copy(
@@ -159,24 +224,40 @@
                 return ar_in[j, 4, 0, :, 0 : self.lanes]
             return None
 
-    def product_slab(low, base):
-        def run(put):
-            step = min(8, slab)
-
-            def body(g, _):
-                block = jnp.concatenate([w[base + g * step + i] for i in range(step)], 1)
-                out = fast(low, block)
-                for i in range(step):
-                    put(g * step + i, out[:, i * LANES : (i + 1) * LANES])
-                return 0
-
-            lax.fori_loop(0, slab // step, body, 0)
-        return run
+    chunk = min(8, slab)
+
+    def product_slab(low, base, put):
+        def body(g, _):
+            block = jnp.concatenate([w[base + g * chunk + i] for i in range(chunk)], 1)
+            out = fast(low, block)
+            for i in range(chunk):
+                put(g * chunk + i, out[:, i * LANES : (i + 1) * LANES])
+            return 0
+
+        lax.fori_loop(0, slab // chunk, body, 0)
 
     def base_of(c, zz):
         return (c * NZ + zz) * slab
 
-    pltpu.make_async_copy(weight_ref, w, load_sem).wait()
+    def arrive(i, _):
+        for dx in range(NX):
+            if dx == 0:
+                @pl.when(i != 0)
+                def _():
+                    block_copy(i, dx).wait()
+            else:
+                block_copy(i, dx).wait()
+        return 0
+
+    lax.fori_loop(0, groups, arrive, 0)
+    pltpu.make_async_copy(staged.at[0, x], w.at[place], keep_sem).wait()
+
+    def keep(p, _):
+        dr, dl = device(p // (NZ * slab), (p // slab) % NZ, (p // NX) % ny, p % NX)
+        pltpu.make_async_copy(w.at[p], blocks_ref.at[dr * (NZ * NYL * NC) + dl], keep_sem).start()
+        return 0
+
+    lax.fori_loop(0, n, keep, 0)
 
     raw[...] = start_ref[...]
     coef_ref[...] = jnp.zeros_like(coef_ref)
@@ -195,23 +276,70 @@
         for d in z_order:
             def put(i, value, d=d):
                 core_out[d, i] = value.astype(BF16)
-            product_slab(low, base_of(1 - core, (z + d) % NZ))(put)
+            product_slab(low, base_of(1 - core, (z + d) % NZ), put)
             core_copies[d] = swap(core_out.at[d], core_in.at[j, d], j, RSC, d)
         reduce.step()
-        z_copies = []
+        flights = [[] for _ in STREAMS]
+
+        def first(t, d):
+            axis = STREAMS[t][2][0]
+            flights[t].append(send(out1[t].at[(here[axis] + d) % sizes[axis]], in1[t].at[j, d - 1],
+                                   j, RS + t, d, axis))
+
         for d in z_order:
-            def put(i, value):
-                acc[i] = value
-            product_slab(low, base_of(core, (z + d) % NZ))(put)
             core_copies[d].wait_recv()
+            at = {"z": (z + d) % NZ}
+
+            def put(i, value, d=d, at=at):
+                value = value + core_in[j, d, i].astype(F32)
+                at = {"z": at["z"], "y": i // NX, "x": i % NX}
+                acc[at["z"] * slab + i] = value
+                for t, (lo, hi, (p, q, r)) in enumerate(STREAMS):
+                    out1[t][at[p], at[q] * sizes[r] + at[r]] = value[lo:hi].astype(BF16)
+
+            product_slab(low, base_of(core, at["z"]), put)
             if d:
-                z_out[d - 1] = (acc[...] + core_in[j, d].astype(F32)).astype(BF16)
-                z_copies.append(send(z_out.at[d - 1], z_in.at[j, d - 1], j, RSZ, d, "z"))
-            else:
-                acc[...] = acc[...] + core_in[j, d].astype(F32)
-        done += list(core_copies.values()) + z_copies
+                first(0, d)
+        for t in (1, 2):
+            for d in range(1, sizes[STREAMS[t][2][0]]):
+                first(t, d)
+        done += list(core_copies.values())
         reduce.step()
+        second = [[] for _ in STREAMS]
+        for t in (1, 2, 0):
+            lo, hi, (p, q, r) = STREAMS[t]
+            for copy in flights[t]:
+                copy.wait_recv()
+
+            def add(iq, _):
+                for ir in range(sizes[r]):
+                    at = {p: here[p], q: iq, r: ir}
+                    value = acc[(at["z"] * ny + at["y"]) * NX + at["x"], lo:hi]
+                    for i in range(sizes[p] - 1):
+                        value = value + in1[t][j, i, iq * sizes[r] + ir].astype(F32)
+                    out2[t][iq, ir] = value
+                return 0
+
+            lax.fori_loop(0, sizes[q], add, 0)
+            for d in range(1, sizes[q]):
+                second[t].append(send(out2[t].at[(here[q] + d) % sizes[q]], in2[t].at[j, d - 1],
+                                      j, RS + 3 + t, d, q))
+            done += flights[t]
         reduce.step()
+        third = [[] for _ in STREAMS]
+        for t in (1, 2, 0):
+            lo, hi, (p, q, r) = STREAMS[t]
+            for copy in second[t]:
+                copy.wait_recv()
+            for ir in range(sizes[r]):
+                value = out2[t][here[q], ir]
+                for i in range(sizes[q] - 1):
+                    value = value + in2[t][j, i, ir]
+                out3[t][ir] = value
+            for d in range(1, sizes[r]):
+                third[t].append(send(out3[t].at[(here[r] + d) % sizes[r]], in3[t].at[j, d - 1],
+                                     j, RS + 6 + t, d, r))
+            done += second[t]
         reduce.step()
         total = reduce.step()
         done += reduce.sent
@@ -222,96 +350,74 @@
             gram_ref[(j - 1) * B : j * B, 0 : j * B] = total[:, (j + 1) * B : (2 * j + 1) * B]
             clean = clean - dot(cross, cross, NT)
         solve = inverse_factor(clean)
+
+        parts = []
+        for t in range(len(STREAMS)):
+            lo, hi, (p, q, r) = STREAMS[t]
+            value = out3[t][here[r]]
+            for i, copy in enumerate(third[t]):
+                copy.wait_recv()
+                value = value + in3[t][j, i]
+            parts.append(value)
+            done += third[t]
+        mine = jnp.concatenate(parts, 0)
+        if j:
+            mine = mine - dot(cross, own[0 : j * B, :])
+        mine = dot(solve, mine)
+        own[j * B : (j + 1) * B, :] = mine
+
+        gathered[j, core, z, y, x] = mine.astype(BF16)
+
+        def spread(t, phase):
+            lo, hi, (p, q, r) = STREAMS[t]
+            axis = (r, q, p)[phase]
+            free = ("", r, r + q)[phase]
+            at = [pl.ds(0, sizes[a]) if a in free else here[a] for a in "zyx"]
+            piece = gathered.at[j, core, at[0], at[1], at[2], pl.ds(lo, hi - lo)]
+            return [send(piece, piece, j, AG + 3 * phase + t, d, axis) for d in range(1, sizes[axis])]
+
+        flights = [spread(t, 0) for t in range(len(STREAMS))]
         block = raw[...]
         if j:
             block = block - dot(cross, right[0 : j * B, :])
         right[j * B : (j + 1) * B, :] = dot(solve, block)
-
-        for copy in z_copies:
-            copy.wait_recv()
-        y_copies = []
-        for d in range(1, ny + 1):
-            e = d % ny
-            at = pl.ds(((y + e) % ny) * NX, NX)
-            value = acc[at]
-            for i in range(NZ - 1):
-                value = value + z_in[j, i, at].astype(F32)
-            if e:
-                y_out[e - 1] = value
-                y_copies.append(send(y_out.at[e - 1], y_in.at[j, e - 1], j, RSY, e, "y"))
-            else:
-                acc[at] = value
-        for copy in y_copies:
-            copy.wait_recv()
-        x_copies = []
-        for d in range(1, NX + 1):
-            e = d % NX
-            at = (x + e) % NX
-            value = acc[y * NX + at]
-            for i in range(ny - 1):
-                value = value + y_in[j, i, at]
-            if e:
-                x_out[e - 1] = value
-                x_copies.append(send(x_out.at[e - 1], x_in.at[j, e - 1], j, RSX, e, "x"))
-            else:
-                mine = value
-        for i, copy in enumerate(x_copies):
-            copy.wait_recv()
-            mine = mine + x_in[j, i]
-        done += y_copies + x_copies
-        if j:
-            mine = mine - dot(cross, own[0 : j * B, :])
-        mine = dot(solve, mine)
-        own[j * B : (j + 1) * B, :] = mine
-
-        place = ((core * NZ + z) * ny + y) * NX + x
-        gathered[j, place] = mine.astype(BF16)
-
-        def spread(axis, phase, at, n):
-            piece = gathered.at[j, pl.ds(at, n)]
-            return [send(piece, piece, j, phase, d, axis) for d in range(1, sizes[axis])]
-
-        for axis, phase, at, n in (("x", AGX, place, 1), ("y", AGY, place - x, NX)):
-            copies = spread(axis, phase, at, n)
-            for copy in copies:
+        for phase in (1, 2):
+            for t in (0, 1, 2):
+                for copy in flights[t]:
+                    copy.wait_recv()
+                done += flights[t]
+                flights[t] = spread(t, phase)
+        for t in (1, 2, 0):
+            for copy in flights[t]:
                 copy.wait_recv()
-            done += copies
-        copies = spread("z", AGZ, base_of(core, z), slab)
-        done += copies
-
-        def back_slab(carry, base):
-            step = min(8, slab)
-
+            done += flights[t]
+        handed = []
+        for d in range(NZ):
+            piece = gathered.at[j, core, (z + d) % NZ]
+            handed.append(swap(piece, piece, j, AGC, d))
+        done += handed
+
+        def back_slab(carry, c, zz):
             def body(g, carry):
                 image, gram = carry
-                pieces = [gathered[j, base + g * step + i] for i in range(step)]
-                newest = jnp.concatenate(pieces, 1)
-                block = jnp.concatenate([w[base + g * step + i] for i in range(step)], 1)
+                index = [(g * (chunk // NX) + i // NX, i % NX) for i in range(chunk)]
+                newest = jnp.concatenate([gathered[j, c, zz, iy, ix] for iy, ix in index], 1)
+                block = jnp.concatenate([w[base_of(c, zz) + g * chunk + i] for i in range(chunk)], 1)
                 image = image + fast(newest, block, NT)
                 grams = []
                 for k in range(j + 1):
                     piece = newest if k == j else jnp.concatenate(
-                        [gathered[k, base + g * step + i] for i in range(step)], 1)
+                        [gathered[k, c, zz, iy, ix] for iy, ix in index], 1)
                     grams.append(gram[k] + fast(newest, piece, NT))
                 return image, tuple(grams)
 
-            return lax.fori_loop(0, slab // step, body, carry)
-
-        def handed(d):
-            piece = gathered.at[j, pl.ds(base_of(core, (z + d) % NZ), slab)]
-            return swap(piece, piece, j, AGC, d)
+            return lax.fori_loop(0, slab // chunk, body, carry)
 
         carry = (jnp.zeros((B, COLS), F32), tuple(jnp.zeros((B, B), F32) for _ in range(j + 1)))
-        handed_on = {0: handed(0)}
-        carry = back_slab(carry, base_of(core, z))
-        for d in range(1, NZ):
-            copies[d - 1].wait_recv()
-            handed_on[(NZ - d) % NZ] = handed((NZ - d) % NZ)
-            carry = back_slab(carry, base_of(core, (z + NZ - d) % NZ))
-        for d in [0] + [(NZ - d) % NZ for d in range(1, NZ)]:
-            handed_on[d].wait_recv()
-            carry = back_slab(carry, base_of(1 - core, (z + d) % NZ))
-        done += list(handed_on.values())
+        carry = lax.fori_loop(0, NZ, lambda zz, carry: back_slab(carry, core, zz), carry)
+        for d in range(NZ):
+            handed[d].wait_recv()
+            carry = back_slab(carry, 1 - core, (z + d) % NZ)
         image, grams = carry
 
         clean = grams[j]
@@ -342,48 +448,61 @@
     gram_ref[(STEPS - 1) * B :, :] = total
     for copy in reduce.sent:
         copy.wait_send()
-
-
-def chain(start_t, blocks):
+    pltpu.make_async_copy(w, blocks_ref, keep_sem).wait()
+
+
+def chain(start_t, weight):
     ny = NYH * NYL
     slab = ny * NX
     n = NC * NZ * slab
     vmem = pl.BlockSpec(memory_space=pltpu.VMEM)
+    hbm = pl.BlockSpec(memory_space=pl.ANY)
     s = STEPS * B
+    sizes = {"z": NZ, "y": ny, "x": NX}
+
+    def buffers(shape, kind):
+        return [pltpu.VMEM(shape(*(sizes[a] for a in axes)) + (hi - lo, LANES), kind) for lo, hi, axes in STREAMS]
+
     return pl.pallas_call(
         chain_kernel,
         out_shape=(
-            jax.ShapeDtypeStruct((STEPS, n, B, LANES), BF16),
+            jax.ShapeDtypeStruct((STEPS, NC, NZ, ny, NX, B, LANES), BF16),
             jax.ShapeDtypeStruct((s, LANES), F32),
             jax.ShapeDtypeStruct((s, COLS), F32),
             jax.ShapeDtypeStruct((s, s), F32),
             jax.ShapeDtypeStruct((s, s), F32),
+            jax.ShapeDtypeStruct((n, COLS, LANES), BF16),
         ),
-        in_specs=[vmem, pl.BlockSpec(memory_space=pl.ANY)],
-        out_specs=[vmem] * 5,
+        in_specs=[vmem, hbm],
+        out_specs=[vmem] * 5 + [hbm],
         scratch_shapes=[
             pltpu.VMEM((n, COLS, LANES), BF16),
+            pltpu.VMEM((2, ROWS, NX * COLS), BF16),
+            pltpu.VMEM((n // NX, NX, COLS, LANES), BF16),
             pltpu.VMEM((NZ, slab, B, LANES), BF16),
             pltpu.VMEM((STEPS, NZ, slab, B, LANES), BF16),
-            pltpu.VMEM((NZ - 1, slab, B, LANES), BF16),
-            pltpu.VMEM((STEPS, NZ - 1, slab, B, LANES), BF16),
-            pltpu.VMEM((ny - 1, NX, B, LANES), F32),
-            pltpu.VMEM((STEPS, ny - 1, NX, B, LANES), F32),
-            pltpu.VMEM((NX - 1, B, LANES), F32),
-            pltpu.VMEM((STEPS, NX - 1, B, LANES), F32),
-            pltpu.VMEM((slab, B, LANES), F32),
+            buffers(lambda p, q, r: (p, q * r), BF16),
+            buffers(lambda p, q, r: (STEPS, max(p - 1, 1), q * r), BF16),
+            buffers(lambda p, q, r: (q, r), F32),
+            buffers(lambda p, q, r: (STEPS, max(q - 1, 1), r), F32),
+            buffers(lambda p, q, r: (r,), F32),
+            buffers(lambda p, q, r: (STEPS, max(r - 1, 1)), F32),
+            pltpu.VMEM((NZ * slab, B, LANES), F32),
             pltpu.VMEM((STEPS + 1, 4, B, 3 * LANES), F32),
             pltpu.VMEM((STEPS + 1, 5, 3, B, 3 * LANES), F32),
             pltpu.VMEM((s, COLS), F32),
             pltpu.VMEM((B, COLS), F32),
             pltpu.VMEM((s, LANES), F32),
+            pltpu.SemaphoreType.DMA((2,)),
             pltpu.SemaphoreType.DMA,
-            pltpu.SemaphoreType.DMA((STEPS + 1, 13, 4)),
-            pltpu.SemaphoreType.DMA((STEPS + 1, 13, 4)),
+            pltpu.SemaphoreType.DMA((n // NX, NX)),
+            pltpu.SemaphoreType.DMA((n // NX, NX)),
+            pltpu.SemaphoreType.DMA((STEPS + 1, EXCHANGES, 4)),
+            pltpu.SemaphoreType.DMA((STEPS + 1, EXCHANGES, 4)),
         ],
         compiler_params=pltpu.CompilerParams(
-            collective_id=0, has_side_effects=True, vmem_limit_bytes=60 * 1024 * 1024),
-    )(start_t, blocks)
+            collective_id=0, has_side_effects=True, vmem_limit_bytes=62 * 1024 * 1024),
+    )(start_t, weight)
 
 
 def sweep_kernel(gram_ref, coef_ref, basis_ref, high_ref, low_ref):
@@ -429,14 +548,13 @@
 
 
 def residual_kernel(gathered, high, low, right, weight, out):
-    ny = NYH * NYL
     first = pl.program_id(0) * PER
     pieces = []
     for i in range(PER):
         at = first + i
         r, c = at // (NZ * NYL * NC), at % (NZ * NYL * NC)
-        place = (((c % NC) * NZ + c // (NYL * NC)) * ny + (r // NX) * NYL + (c // NC) % NYL) * NX + r % NX
-        pieces.append(jnp.concatenate([gathered[k, place] for k in range(STEPS)], 0))
+        place = (c % NC, c // (NYL * NC), (r // NX) * NYL + (c // NC) % NYL, r % NX)
+        pieces.append(jnp.concatenate([gathered[(k,) + place] for k in range(STEPS)], 0))
     stacked = jnp.concatenate(pieces, 1)
     left = (fast(high[...], stacked) + fast(low[...], stacked)).astype(BF16).T
     left = jnp.concatenate([left[i * LANES : i * LANES + ROWS] for i in range(PER)], 0)
@@ -468,12 +586,7 @@
 
 
 def shards(weight, start):
-    rows, cols = NYH * NX, NZ * NYL * NC
-    n = rows * cols
-    padded = jnp.pad(weight, ((0, LANES - ROWS), (0, 0)))
-    parts = padded.T.reshape(cols, rows, COLS, LANES).transpose(1, 0, 2, 3).reshape(n, COLS, LANES)
-    blocks = lax.all_to_all(parts, ("row", "col"), split_axis=0, concat_axis=0, tiled=True)
-    gathered, left, images, gram, coef = chain(start.T, blocks)
+    gathered, left, images, gram, coef, blocks = chain(start.T, weight)
     basis, high, low = sweeps(gram, coef)
     adapter_left = lax.dot_general(left[:, :ROWS], basis, (((0,), (1,)), ((), ())), precision=HIGHEST,
                                    preferred_element_type=F32)

time: 468 us -> 397 us (0.85)
  blocking collectives: 171 us -> 0 us
  Pallas kernels: 263 us -> 388 us
  local copies, waits for them, and re-layouts: 26.7 us -> 1.68 us
    all_to_all x1 -> x0, blocking collectives: 171 us -> none  [shards(): lax.all_to_all(parts, ('row', 'col'), split_axis=0, concat_axis=0, tiled=...]
    pallas_call x1, Pallas kernels: 221 us -> 346 us  [chain(): pl.pallas_call(chain_kernel, out_shape=(jax.ShapeDtypeStruct((STEPS, NC,...]
    unnamed x5 -> x4, local copies, waits for them, and re-layouts: 18.6 us -> 1.68 us
    pad x1 -> x0, local copies, waits for them, and re-layouts: 6.18 us -> none  [shards(): padded = jnp.pad(weight, ((0, LANES - ROWS), (0, 0)))]
where the time goes in v3:
time: 397 us; the launch traced here: 395 us
  Pallas kernels  388 us (98%)
  matrix products  4.66 us (1%)
    pallas_call x1, Pallas kernels, chain(): pl.pallas_call(chain_kernel, out_shape=(jax.ShapeDtypeStruct((STEPS, NC,...  346 us
    pallas_call x1, Pallas kernels, residual(): pl.pallas_call(residual_kernel, grid=(n // PER,), out_shape=jax.ShapeDtyp...  21.7 us
    pallas_call x1, Pallas kernels, sweeps(): pl.pallas_call(sweep_kernel, out_shape=(jax.ShapeDtypeStruct((RANK, s), F...  20.4 us

profile of v3, /device:TPU:1, one launch (start us, length us, event | category | flops | bytes accessed | tf_op | source)
XLA Modules:
  0.0 395.3 jit_solution(11836455821408656905)
XLA Ops:
  0.6 346.2 %shard_map.49 = (bf16[3,2,4,4,4,64,128]{6,5,4,3,2,1,0:T(8,128)(2,1)}, f32[192,128]{1,0:T(8,128)}, f32[192,416]{1,0:T(8,128)}, f32[192,192]{1,0:T(8,128)}, f32[19...) custom-call(f32[64,416]{1,0:T(8,128)} %bitcast.6, bf16[112,53248]{1,0:T(8,128)(2,1)} %weight_ref.1), custom_call_target="tpu_custom_call" | custom-call | tf_op jit(solution)/shard_map/pallas_call | solution.py:466
  346.8 20.4 %shard_map.50 = (f32[128,192]{1,0:T(8,128)}, bf16[128,192]{1,0:T(8,128)(2,1)}, bf16[128,192]{1,0:T(8,128)(2,1)}) custom-call(f32[192,192]{1,0:T(8,128)} %get-tuple-element.13.gram_ref, f32[192,192]{1,0:T(8,128)} %get-tuple-element.14.coef_ref), custom_call_target="tpu_custom_call" | custom-call | tf_op jit(solution)/shard_map/pallas_call | solution.py:537
  367.2 2.7 fusion.2
  369.9 2.0 fusion
  371.9 0.0 copy-start
  371.9 0.8 copy-done
  372.7 0.0 copy-start.1
  372.7 0.8 copy-done.1
  373.6 21.7 %shard_map.51 = bf16[416,14336]{1,0:T(8,128)(2,1)} custom-call(bf16[3,2,4,4,4,64,128]{6,5,4,3,2,1,0:T(8,128)(2,1)} %get-tuple-element.17.gathered, bf16[128,192]{1,0:T(8,128)(2,1)S(1)} %copy-done, bf16[128,192]{1,0:T(8,128)(2,1)S(1)} %copy-done.1, bf16[416,128]{1,0:T(8,128)(2,1)S(1)} %get-tuple-element.21.right, bf16[128,416,128]{2,1,0:T(8,128)(2,1)} %get-tuple-element.20.weight), custom_call_target="tpu_custom_call" | custom-call | tf_op jit(solution)/shard_map/pallas_call | solution.py:577
Async XLA Ops:
  371.9 0.8 copy-start
  372.7 0.8 copy-start.1

commit v4 on v3

--- a/solution.py
+++ b/solution.py
@@ -15,6 +15,8 @@
 
 NX, NYH, NYL, NZ, NC = 4, 2, 2, 4, 2
 ROWS, COLS = 112, 416
+GAP, TAIL = LANES - ROWS, 48
+SENT = COLS - TAIL
 
 HIGHEST = lax.Precision.HIGHEST
 MESH = pl.DeviceIdType.MESH
@@ -63,6 +65,28 @@
     return jnp.concatenate(rows, 0)[:, B:]
 
 
+def pack(block):
+    tail = block[SENT:].astype(F32)
+    lane = lax.broadcasted_iota(jnp.int32, (TAIL, LANES), 1)
+    pieces = []
+    for m in range(ROWS // GAP):
+        moved = pltpu.roll(tail, ROWS - GAP * m, 1)
+        pieces.append(jnp.where(lane < ROWS, block[TAIL * m : TAIL * (m + 1)].astype(F32), moved).astype(BF16))
+    return jnp.concatenate(pieces + [block[TAIL * (ROWS // GAP) : SENT]], 0)
+
+
+def unpack(w, p):
+    lane = lax.broadcasted_iota(jnp.int32, (TAIL, LANES), 1)
+    tail = jnp.zeros((TAIL, LANES), F32)
+    for m in range(ROWS // GAP):
+        at = slice(TAIL * m, TAIL * (m + 1))
+        piece = w[p, at].astype(F32)
+        moved = pltpu.roll(piece, (LANES - ROWS + GAP * m) % LANES, 1)
+        tail = jnp.where((lane >= GAP * m) & (lane < GAP * (m + 1)), moved, tail)
+        w[p, at] = jnp.where(lane < ROWS, piece, 0.0).astype(BF16)
+    w[p, SENT:] = tail.astype(BF16)
+
+
 def chain_kernel(start_ref, weight_ref, gathered, left_ref, image_ref, gram_ref, coef_ref, blocks_ref,
                  w, strip, staged, core_out, core_in, out1, in1, out2, in2, out3, in3, acc,
                  ar_out, ar_in, right, raw, own, strip_sem, keep_sem, put_sem, get_sem, send_sem, recv_sem):
@@ -112,7 +136,7 @@
         dc, dz, dy = offset(i)
         tx = (x + dx) % NX
         return pltpu.make_async_remote_copy(
-            src_ref=staged.at[i, tx], dst_ref=w.at[place], send_sem=put_sem.at[i, dx], recv_sem=get_sem.at[i, dx],
+            src_ref=staged.at[i, tx], dst_ref=w.at[place, pl.ds(0, SENT)], send_sem=put_sem.at[i, dx], recv_sem=get_sem.at[i, dx],
             device_id=device((core + dc) % NC, (z + dz) % NZ, (y + dy) % ny, tx), device_id_type=MESH)
 
     strip_copy(0).start()
@@ -135,7 +159,8 @@
 
         value = strip[i % 2]
         value = jnp.concatenate([value, jnp.zeros((LANES - ROWS, NX * COLS), BF16)], 0).T
-        staged[i] = value.reshape(NX, COLS, LANES)
+        for k in range(NX):
+            staged[i, k] = pack(value[k * COLS : (k + 1) * COLS])
 
     def scatter(step, _):
         def each(g, _):
@@ -147,7 +172,7 @@
         @pl.when(step == 0)
         def _():
             pl.semaphore_wait(barrier, n - 1)
-            pltpu.make_async_copy(staged.at[0, x], w.at[place], keep_sem).start()
+            pltpu.make_async_copy(staged.at[0, x], w.at[place, pl.ds(0, SENT)], keep_sem).start()
 
         def rotate(a, _):
             for dx in range(NX):
@@ -224,22 +249,25 @@
                 return ar_in[j, 4, 0, :, 0 : self.lanes]
             return None
 
-    chunk = min(8, slab)
-
     def product_slab(low, base, put):
-        def body(g, _):
-            block = jnp.concatenate([w[base + g * chunk + i] for i in range(chunk)], 1)
-            out = fast(low, block)
-            for i in range(chunk):
-                put(g * chunk + i, out[:, i * LANES : (i + 1) * LANES])
-            return 0
-
-        lax.fori_loop(0, slab // chunk, body, 0)
+        out = fast(low, jnp.concatenate([w[base + i] for i in range(slab)], 1))
+        for i in range(slab):
+            put(i, out[:, i * LANES : (i + 1) * LANES])
 
     def base_of(c, zz):
         return (c * NZ + zz) * slab
 
+    raw[...] = start_ref[...]
+    coef_ref[...] = jnp.zeros_like(coef_ref)
+    start_low = raw[...].astype(BF16)
+    right[0:B, :] = raw[...]
+    reduce = Reduce(dot(raw[...], raw[...], NT), 0)
+    pltpu.make_async_copy(staged.at[0, x], w.at[place, pl.ds(0, SENT)], keep_sem).wait()
+
     def arrive(i, _):
+        dc, dz, dy = offset(i)
+        fz, fy = (z - dz + NZ) % NZ, (y - dy + ny) % ny
+        base = spot((core - dc + NC) % NC, fz, fy, 0)
         for dx in range(NX):
             if dx == 0:
                 @pl.when(i != 0)
@@ -247,10 +275,25 @@
                     block_copy(i, dx).wait()
             else:
                 block_copy(i, dx).wait()
+        for k in range(NX):
+            unpack(w, base + k)
+        out = fast(start_low, jnp.concatenate([w[base + k] for k in range(NX)], 1))
+
+        @pl.when(dc == 0)
+        def _():
+            for k in range(NX):
+                acc[(fz * ny + fy) * NX + k] = out[:, k * LANES : (k + 1) * LANES]
+
+        @pl.when(dc != 0)
+        def _():
+            for k in range(NX):
+                core_out[(NZ - dz) % NZ, fy * NX + k] = out[:, k * LANES : (k + 1) * LANES].astype(BF16)
+
         return 0
 
-    lax.fori_loop(0, groups, arrive, 0)
-    pltpu.make_async_copy(staged.at[0, x], w.at[place], keep_sem).wait()
+    lax.fori_loop(0, groups // NC, arrive, 0)
+    reduce.step()
+    lax.fori_loop(groups // NC, groups, arrive, 0)
 
     def keep(p, _):
         dr, dl = device(p // (NZ * slab), (p // slab) % NZ, (p // NX) % ny, p % NX)
@@ -259,26 +302,25 @@
 
     lax.fori_loop(0, n, keep, 0)
 
-    raw[...] = start_ref[...]
-    coef_ref[...] = jnp.zeros_like(coef_ref)
     z_order = [d % NZ for d in range(1, NZ + 1)]
     for j in range(STEPS):
         done = []
         low = raw[...].astype(BF16)
-        right[j * B : (j + 1) * B, :] = raw[...]
-        gram = dot(raw[...], right[0 : (j + 1) * B, :], NT)
-        if j:
+        if j:
+            right[j * B : (j + 1) * B, :] = raw[...]
+            gram = dot(raw[...], right[0 : (j + 1) * B, :], NT)
             newest = image_ref[(j - 1) * B : j * B, :]
-            gram = jnp.concatenate([gram, dot(newest, image_ref[0 : j * B, :], NT)], 1)
-        reduce = Reduce(gram, j)
+            reduce = Reduce(jnp.concatenate([gram, dot(newest, image_ref[0 : j * B, :], NT)], 1), j)
 
         core_copies = {}
         for d in z_order:
             def put(i, value, d=d):
                 core_out[d, i] = value.astype(BF16)
-            product_slab(low, base_of(1 - core, (z + d) % NZ), put)
+            if j:
+                product_slab(low, base_of(1 - core, (z + d) % NZ), put)
             core_copies[d] = swap(core_out.at[d], core_in.at[j, d], j, RSC, d)
-        reduce.step()
+        if j:
+            reduce.step()
         flights = [[] for _ in STREAMS]
 
         def first(t, d):
@@ -297,7 +339,11 @@
                 for t, (lo, hi, (p, q, r)) in enumerate(STREAMS):
                     out1[t][at[p], at[q] * sizes[r] + at[r]] = value[lo:hi].astype(BF16)
 
-            product_slab(low, base_of(core, at["z"]), put)
+            if j:
+                product_slab(low, base_of(core, at["z"]), put)
+            else:
+                for i in range(slab):
+                    put(i, acc[at["z"] * slab + i])
             if d:
                 first(0, d)
         for t in (1, 2):
@@ -397,33 +443,29 @@
             handed.append(swap(piece, piece, j, AGC, d))
         done += handed
 
-        def back_slab(carry, c, zz):
-            def body(g, carry):
-                image, gram = carry
-                index = [(g * (chunk // NX) + i // NX, i % NX) for i in range(chunk)]
-                newest = jnp.concatenate([gathered[j, c, zz, iy, ix] for iy, ix in index], 1)
-                block = jnp.concatenate([w[base_of(c, zz) + g * chunk + i] for i in range(chunk)], 1)
-                image = image + fast(newest, block, NT)
-                grams = []
-                for k in range(j + 1):
-                    piece = newest if k == j else jnp.concatenate(
-                        [gathered[k, c, zz, iy, ix] for iy, ix in index], 1)
-                    grams.append(gram[k] + fast(newest, piece, NT))
-                return image, tuple(grams)
-
-            return lax.fori_loop(0, slab // chunk, body, carry)
-
-        carry = (jnp.zeros((B, COLS), F32), tuple(jnp.zeros((B, B), F32) for _ in range(j + 1)))
-        carry = lax.fori_loop(0, NZ, lambda zz, carry: back_slab(carry, core, zz), carry)
-        for d in range(NZ):
-            handed[d].wait_recv()
-            carry = back_slab(carry, 1 - core, (z + d) % NZ)
-        image, grams = carry
-
-        clean = grams[j]
+        def back_slab(total, c, zz):
+            wide = [jnp.concatenate([w[base_of(c, zz) + i] for i in range(slab)], 1)]
+            for k in range(j + 1):
+                wide.append(jnp.concatenate([gathered[k, c, zz, i // NX, i % NX] for i in range(slab)], 1))
+            return total + fast(wide[-1], jnp.concatenate(wide, 0), NT)
+
+        total = jnp.zeros((B, COLS + (j + 1) * B), F32)
+        total = lax.fori_loop(0, NZ, lambda zz, total: back_slab(total, core, zz), total)
+
+        def handed_in(d, total):
+            piece = gathered.at[j, core, (z + d) % NZ]
+            pltpu.make_async_remote_copy(
+                src_ref=piece, dst_ref=piece, send_sem=send_sem.at[j, AGC, d], recv_sem=recv_sem.at[j, AGC, d],
+                device_id=peer("c", 1), device_id_type=MESH).wait_recv()
+            return back_slab(total, 1 - core, (z + d) % NZ)
+
+        total = lax.fori_loop(0, NZ, handed_in, total)
+        image, grams = total[:, :COLS], total[:, COLS:]
+
+        clean = grams[:, j * B :]
         if j:
             table = coef_ref[0 : j * B, 0 : j * B]
-            cross = dot(jnp.concatenate(grams[:j], 1), table, NT)
+            cross = dot(grams[:, : j * B], table, NT)
             clean = clean - dot(cross, cross, NT)
         solve = inverse_factor(clean)
         if j:
@@ -478,7 +520,7 @@
         scratch_shapes=[
             pltpu.VMEM((n, COLS, LANES), BF16),
             pltpu.VMEM((2, ROWS, NX * COLS), BF16),
-            pltpu.VMEM((n // NX, NX, COLS, LANES), BF16),
+            pltpu.VMEM((n // NX, NX, SENT, LANES), BF16),
             pltpu.VMEM((NZ, slab, B, LANES), BF16),
             pltpu.VMEM((STEPS, NZ, slab, B, LANES), BF16),
             buffers(lambda p, q, r: (p, q * r), BF16),
@@ -505,7 +547,7 @@
     )(start_t, weight)
 
 
-def sweep_kernel(gram_ref, coef_ref, basis_ref, high_ref, low_ref):
+def sweep_kernel(gram_ref, coef_ref, left_ref, image_ref, adapter_left, adapter_right, low_right, high_ref, low_ref):
     g = [[None] * STEPS for _ in range(STEPS)]
     for i in range(STEPS):
         for k in range(i + 1):
@@ -525,23 +567,28 @@
 
     basis = orth(whole[:RANK])
     basis = lax.fori_loop(1, SWEEPS, lambda _, basis: orth(dot(basis, whole)), basis)
-    basis_ref[...] = basis
+    adapter_left[...] = dot(basis, left_ref[...]).T[:ROWS]
+    wide = dot(basis, image_ref[...]).T
+    adapter_right[...] = wide
+    low_right[...] = wide.astype(BF16)
     mixed = dot(basis, coef_ref[...])
     high = mixed.astype(BF16)
     high_ref[...] = high
     low_ref[...] = (mixed - high.astype(F32)).astype(BF16)
 
 
-def sweeps(gram, coef):
+def sweeps(gram, coef, left, images):
     s = STEPS * B
     return pl.pallas_call(
         sweep_kernel,
         out_shape=(
-            jax.ShapeDtypeStruct((RANK, s), F32),
+            jax.ShapeDtypeStruct((ROWS, RANK), F32),
+            jax.ShapeDtypeStruct((COLS, RANK), F32),
+            jax.ShapeDtypeStruct((COLS, RANK), BF16),
             jax.ShapeDtypeStruct((RANK, s), BF16),
             jax.ShapeDtypeStruct((RANK, s), BF16),
         ),
-    )(gram, coef)
+    )(gram, coef, left, images)
 
 
 PER = 8
@@ -587,12 +634,8 @@
 
 def shards(weight, start):
     gathered, left, images, gram, coef, blocks = chain(start.T, weight)
-    basis, high, low = sweeps(gram, coef)
-    adapter_left = lax.dot_general(left[:, :ROWS], basis, (((0,), (1,)), ((), ())), precision=HIGHEST,
-                                   preferred_element_type=F32)
-    adapter_right = lax.dot_general(images, basis, (((0,), (1,)), ((), ())), precision=HIGHEST,
-                                    preferred_element_type=F32)
-    out = residual(gathered, high, low, adapter_right.astype(BF16), blocks)
+    adapter_left, adapter_right, low_right, high, low = sweeps(gram, coef, left, images)
+    out = residual(gathered, high, low, low_right, blocks)
     return (adapter_left, adapter_right, out.T)
 
 

time: 397 us -> 369 us (0.929)
  Pallas kernels: 388 us -> 364 us
  matrix products: 4.66 us -> 0 us
    pallas_call x1, Pallas kernels: 346 us -> 321 us  [chain(): pl.pallas_call(chain_kernel, out_shape=(jax.ShapeDtypeStruct((STEPS, NC,...]
    dot_general x2 -> x0, matrix products: 4.66 us -> none  [the longest x1 2.68 us: shards(): lax.dot_general(images, basis, (((0,), (1,)), ((), ())), precision=HIGHES...]
where the time goes in v4:
time: 369 us; the launch traced here: 367 us
  Pallas kernels  364 us (99%)
    pallas_call x1, Pallas kernels, chain(): pl.pallas_call(chain_kernel, out_shape=(jax.ShapeDtypeStruct((STEPS, NC,...  321 us
    pallas_call x1, Pallas kernels, residual(): pl.pallas_call(residual_kernel, grid=(n // PER,), out_shape=jax.ShapeDtyp...  21.7 us
    pallas_call x1, Pallas kernels, sweeps(): pl.pallas_call(sweep_kernel, out_shape=(jax.ShapeDtypeStruct((ROWS, RANK)...  21.1 us

profile of v4, /device:TPU:1, one launch (start us, length us, event | category | flops | bytes accessed | tf_op | source)
XLA Modules:
  0.0 366.9 jit_solution(13890484916582162982)
XLA Ops:
  0.6 320.9 %shard_map.49 = (bf16[3,2,4,4,4,64,128]{6,5,4,3,2,1,0:T(8,128)(2,1)}, f32[192,128]{1,0:T(8,128)}, f32[192,416]{1,0:T(8,128)}, f32[192,192]{1,0:T(8,128)}, f32[19...) custom-call(f32[64,416]{1,0:T(8,128)} %bitcast.3, bf16[112,53248]{1,0:T(8,128)(2,1)} %weight_ref.1), custom_call_target="tpu_custom_call" | custom-call | tf_op jit(solution)/shard_map/pallas_call | solution.py:508
  321.5 21.1 %shard_map.50 = (f32[112,128]{1,0:T(8,128)}, f32[416,128]{1,0:T(8,128)}, bf16[416,128]{1,0:T(8,128)(2,1)}, bf16[128,192]{1,0:T(8,128)(2,1)}, bf16[128,192]{1,0:T(8,128)(2,1)}) custom-call(f32[192,192]{1,0:T(8,128)} %get-tuple-element.14.gram_ref, f32[192,192]{1,0:T(8,128)} %get-tuple-element.15.coef_ref, f32[192,128]{1,0:T(8,128)} %get-tuple-element.16.left_ref, ...), custom_call_target="tpu_custom_call" | custom-call | tf_op jit(solution)/shard_map/pallas_call | solution.py:582
  342.6 0.0 copy-start
  342.6 0.9 copy-done
  343.5 0.0 copy-start.1
  343.5 0.8 copy-done.1
  344.3 0.0 copy-start.2
  344.3 0.8 copy-done.2
  345.2 21.7 %shard_map.51 = bf16[416,14336]{1,0:T(8,128)(2,1)} custom-call(bf16[3,2,4,4,4,64,128]{6,5,4,3,2,1,0:T(8,128)(2,1)} %get-tuple-element.20.gathered, bf16[128,192]{1,0:T(8,128)(2,1)S(1)} %copy-done.1, bf16[128,192]{1,0:T(8,128)(2,1)S(1)} %copy-done.2, bf16[416,128]{1,0:T(8,128)(2,1)S(1)} %copy-done, bf16[128,416,128]{2,1,0:T(8,128)(2,1)} %get-tuple-element.24.weight), custom_call_target="tpu_custom_call" | custom-call | tf_op jit(solution)/shard_map/pallas_call | solution.py:624
Async XLA Ops:
  342.6 0.9 copy-start
  343.5 0.8 copy-start.1
  344.3 0.8 copy-start.2

commit v5 on v4

--- a/solution.py
+++ b/solution.py
@@ -9,6 +9,7 @@
 
 STEPS = 3
 RANK = 128
+PER = 8
 SWEEPS = 4
 B = 64
 LANES = 128
@@ -89,7 +90,7 @@
 
 def chain_kernel(start_ref, weight_ref, gathered, left_ref, image_ref, gram_ref, coef_ref, blocks_ref,
                  w, strip, staged, core_out, core_in, out1, in1, out2, in2, out3, in3, acc,
-                 ar_out, ar_in, right, raw, own, strip_sem, keep_sem, put_sem, get_sem, send_sem, recv_sem):
+                 ar_out, ar_in, right, raw, own, joined, join_sem, strip_sem, keep_sem, put_sem, get_sem, send_sem, recv_sem):
     ny = NYH * NYL
     slab = ny * NX
     n = NC * NZ * slab
@@ -295,12 +296,38 @@
     reduce.step()
     lax.fori_loop(groups // NC, groups, arrive, 0)
 
-    def keep(p, _):
-        dr, dl = device(p // (NZ * slab), (p // slab) % NZ, (p // NX) % ny, p % NX)
-        pltpu.make_async_copy(w.at[p], blocks_ref.at[dr * (NZ * NYL * NC) + dl], keep_sem).start()
+    lane = lax.broadcasted_iota(jnp.int32, (COLS, LANES), 1)
+    spans = n // PER
+
+    def joined_copy(i):
+        return pltpu.make_async_copy(
+            joined.at[i % 2], blocks_ref.at[:, pl.ds(pl.multiple_of(i * PER * ROWS, LANES), PER * ROWS)],
+            join_sem.at[i % 2])
+
+    def join(i, _):
+        @pl.when(i >= 2)
+        def _():
+            joined_copy(i - 2).wait()
+
+        parts = []
+        for k in range(PER):
+            at = i * PER + k
+            r, c = at // (NZ * NYL * NC), at % (NZ * NYL * NC)
+            parts.append(spot(c % NC, c // (NYL * NC), (r // NX) * NYL + (c // NC) % NYL, r % NX))
+        for t in range(PER * ROWS // LANES):
+            first = w[parts[t]].astype(F32)
+            if t:
+                first = pltpu.roll(first, LANES - GAP * t, 1)
+            after = pltpu.roll(w[parts[t + 1]].astype(F32), ROWS - GAP * t, 1)
+            joined[i % 2, :, t * LANES : (t + 1) * LANES] = jnp.where(lane < ROWS - GAP * t, first, after).astype(BF16)
+        joined_copy(i).start()
         return 0
 
-    lax.fori_loop(0, n, keep, 0)
+    quota = iter([(i * spans // (2 * STEPS), (i + 1) * spans // (2 * STEPS)) for i in range(2 * STEPS)])
+
+    def fill():
+        lo, hi = next(quota)
+        lax.fori_loop(lo, hi, join, 0)
 
     z_order = [d % NZ for d in range(1, NZ + 1)]
     for j in range(STEPS):
@@ -350,6 +377,8 @@
             for d in range(1, sizes[STREAMS[t][2][0]]):
                 first(t, d)
         done += list(core_copies.values())
+        reduce.step()
+        fill()
         reduce.step()
         second = [[] for _ in STREAMS]
         for t in (1, 2, 0):
@@ -386,7 +415,6 @@
                 third[t].append(send(out3[t].at[(here[r] + d) % sizes[r]], in3[t].at[j, d - 1],
                                      j, RS + 6 + t, d, r))
             done += second[t]
-        reduce.step()
         total = reduce.step()
         done += reduce.sent
 
@@ -433,6 +461,7 @@
                     copy.wait_recv()
                 done += flights[t]
                 flights[t] = spread(t, phase)
+        fill()
         for t in (1, 2, 0):
             for copy in flights[t]:
                 copy.wait_recv()
@@ -490,7 +519,8 @@
     gram_ref[(STEPS - 1) * B :, :] = total
     for copy in reduce.sent:
         copy.wait_send()
-    pltpu.make_async_copy(w, blocks_ref, keep_sem).wait()
+    joined_copy(spans - 2).wait()
+    joined_copy(spans - 1).wait()
 
 
 def chain(start_t, weight):
@@ -513,7 +543,7 @@
             jax.ShapeDtypeStruct((s, COLS), F32),
             jax.ShapeDtypeStruct((s, s), F32),
             jax.ShapeDtypeStruct((s, s), F32),
-            jax.ShapeDtypeStruct((n, COLS, LANES), BF16),
+            jax.ShapeDtypeStruct((COLS, n * ROWS), BF16),
         ),
         in_specs=[vmem, hbm],
         out_specs=[vmem] * 5 + [hbm],
@@ -535,6 +565,8 @@
             pltpu.VMEM((s, COLS), F32),
             pltpu.VMEM((B, COLS), F32),
             pltpu.VMEM((s, LANES), F32),
+            pltpu.VMEM((2, COLS, PER * ROWS), BF16),
+            pltpu.SemaphoreType.DMA((2,)),
             pltpu.SemaphoreType.DMA((2,)),
             pltpu.SemaphoreType.DMA,
             pltpu.SemaphoreType.DMA((n // NX, NX)),
@@ -547,7 +579,7 @@
     )(start_t, weight)
 
 
-def sweep_kernel(gram_ref, coef_ref, left_ref, image_ref, adapter_left, adapter_right, low_right, high_ref, low_ref):
+def sweeps(gram_ref, coef_ref):
     g = [[None] * STEPS for _ in range(STEPS)]
     for i in range(STEPS):
         for k in range(i + 1):
@@ -566,76 +598,57 @@
         return jnp.concatenate([first, dot(two, clean)], 0)
 
     basis = orth(whole[:RANK])
-    basis = lax.fori_loop(1, SWEEPS, lambda _, basis: orth(dot(basis, whole)), basis)
-    adapter_left[...] = dot(basis, left_ref[...]).T[:ROWS]
-    wide = dot(basis, image_ref[...]).T
-    adapter_right[...] = wide
-    low_right[...] = wide.astype(BF16)
-    mixed = dot(basis, coef_ref[...])
-    high = mixed.astype(BF16)
-    high_ref[...] = high
-    low_ref[...] = (mixed - high.astype(F32)).astype(BF16)
-
-
-def sweeps(gram, coef, left, images):
-    s = STEPS * B
-    return pl.pallas_call(
-        sweep_kernel,
-        out_shape=(
-            jax.ShapeDtypeStruct((ROWS, RANK), F32),
-            jax.ShapeDtypeStruct((COLS, RANK), F32),
-            jax.ShapeDtypeStruct((COLS, RANK), BF16),
-            jax.ShapeDtypeStruct((RANK, s), BF16),
-            jax.ShapeDtypeStruct((RANK, s), BF16),
-        ),
-    )(gram, coef, left, images)
-
-
-PER = 8
-
-
-def residual_kernel(gathered, high, low, right, weight, out):
-    first = pl.program_id(0) * PER
+    return lax.fori_loop(1, SWEEPS, lambda _, basis: orth(dot(basis, whole)), basis)
+
+
+def finish_kernel(gram_ref, coef_ref, left_ref, image_ref, gathered, weight,
+                  adapter_left, adapter_right, out, high, low, right):
+    @pl.when(pl.program_id(0) == 0)
+    def _():
+        basis = sweeps(gram_ref, coef_ref)
+        adapter_left[...] = dot(basis, left_ref[...]).T[:ROWS]
+        wide = dot(basis, image_ref[...]).T
+        adapter_right[...] = wide
+        right[...] = wide.astype(BF16)
+        mixed = dot(basis, coef_ref[...])
+        high[...] = mixed.astype(BF16)
+        low[...] = (mixed - mixed.astype(BF16).astype(F32)).astype(BF16)
+
     pieces = []
     for i in range(PER):
-        at = first + i
+        at = pl.program_id(0) * PER + i
         r, c = at // (NZ * NYL * NC), at % (NZ * NYL * NC)
         place = (c % NC, c // (NYL * NC), (r // NX) * NYL + (c // NC) % NYL, r % NX)
         pieces.append(jnp.concatenate([gathered[(k,) + place] for k in range(STEPS)], 0))
     stacked = jnp.concatenate(pieces, 1)
     left = (fast(high[...], stacked) + fast(low[...], stacked)).astype(BF16).T
     left = jnp.concatenate([left[i * LANES : i * LANES + ROWS] for i in range(PER)], 0)
-    update = fast(right[...], left, NT)
-    lane = lax.broadcasted_iota(jnp.int32, (COLS, LANES), 1)
-    gap = LANES - ROWS
-    for t in range(PER * ROWS // LANES):
-        block = weight[t].astype(F32)
-        if t:
-            block = pltpu.roll(block, LANES - gap * t, 1)
-        after = pltpu.roll(weight[t + 1].astype(F32), ROWS - gap * t, 1)
-        block = jnp.where(lane < ROWS - gap * t, block, after)
-        at = slice(t * LANES, (t + 1) * LANES)
-        out[:, at] = (block - update[:, at]).astype(BF16)
-
-
-def residual(gathered, high, low, right, blocks):
-    n = blocks.shape[0]
-    whole = lambda a: pl.BlockSpec(a.shape, lambda i: (0,) * a.ndim)
+    out[...] = (weight[...].astype(F32) - fast(right[...], left, NT)).astype(BF16)
+
+
+def finish(gram, coef, left, images, gathered, blocks):
+    rows = blocks.shape[1]
+    s = STEPS * B
+    whole = lambda shape: pl.BlockSpec(shape, lambda i: (0,) * len(shape))
+    strip = pl.BlockSpec((COLS, PER * ROWS), lambda i: (0, i))
     return pl.pallas_call(
-        residual_kernel,
-        grid=(n // PER,),
-        out_shape=jax.ShapeDtypeStruct((COLS, n * ROWS), BF16),
-        in_specs=[whole(gathered), whole(high), whole(low), whole(right),
-                  pl.BlockSpec((PER, COLS, LANES), lambda i: (i, 0, 0))],
-        out_specs=pl.BlockSpec((COLS, PER * ROWS), lambda i: (0, i)),
+        finish_kernel,
+        grid=(rows // (PER * ROWS),),
+        out_shape=(
+            jax.ShapeDtypeStruct((ROWS, RANK), F32),
+            jax.ShapeDtypeStruct((COLS, RANK), F32),
+            jax.ShapeDtypeStruct((COLS, rows), BF16),
+        ),
+        in_specs=[whole(a.shape) for a in (gram, coef, left, images, gathered)] + [strip],
+        out_specs=(whole((ROWS, RANK)), whole((COLS, RANK)), strip),
+        scratch_shapes=[pltpu.VMEM((RANK, s), BF16), pltpu.VMEM((RANK, s), BF16), pltpu.VMEM((COLS, RANK), BF16)],
         compiler_params=pltpu.CompilerParams(vmem_limit_bytes=48 * 1024 * 1024),
-    )(gathered, high, low, right, blocks)
+    )(gram, coef, left, images, gathered, blocks)
 
 
 def shards(weight, start):
     gathered, left, images, gram, coef, blocks = chain(start.T, weight)
-    adapter_left, adapter_right, low_right, high, low = sweeps(gram, coef, left, images)
-    out = residual(gathered, high, low, low_right, blocks)
+    adapter_left, adapter_right, out = finish(gram, coef, left, images, gathered, blocks)
     return (adapter_left, adapter_right, out.T)
 
 

time: 369 us -> 366 us (level)
  Pallas kernels: 364 us -> 360 us
    pallas_call x2 -> x1, Pallas kernels: 42.8 us -> 40.2 us  [finish(): pl.pallas_call(finish_kernel, grid=(rows // (PER * ROWS),), out_shape=(ja...]
where the time goes in v5:
time: 366 us; the launch traced here: 365 us
  Pallas kernels  360 us (98%)
  local copies, waits for them, and re-layouts  3.73 us (1%)
    pallas_call x1, Pallas kernels, chain(): pl.pallas_call(chain_kernel, out_shape=(jax.ShapeDtypeStruct((STEPS, NC,...  320 us
    pallas_call x1, Pallas kernels, finish(): pl.pallas_call(finish_kernel, grid=(rows // (PER * ROWS),), out_shape=(ja...  40.2 us

profile of v5, /device:TPU:1, one launch (start us, length us, event | category | flops | bytes accessed | tf_op | source)
XLA Modules:
  0.0 364.7 jit_solution(707771575561221720)
XLA Ops:
  0.6 320.1 %shard_map.49 = (bf16[3,2,4,4,4,64,128]{6,5,4,3,2,1,0:T(8,128)(2,1)}, f32[192,128]{1,0:T(8,128)}, f32[192,416]{1,0:T(8,128)}, f32[192,192]{1,0:T(8,128)}, f32[19...) custom-call(f32[64,416]{1,0:T(8,128)} %bitcast.2, bf16[112,53248]{1,0:T(8,128)(2,1)} %weight_ref.1), custom_call_target="tpu_custom_call" | custom-call | tf_op jit(solution)/shard_map/pallas_call | solution.py:538
  320.8 0.0 copy-start
  320.8 1.0 copy-done
  321.8 0.0 copy-start.1
  321.8 0.9 copy-done.1
  322.7 0.0 copy-start.2
  322.7 0.9 copy-done.2
  323.6 0.0 copy-start.3
  323.6 0.9 copy-done.3
  324.5 40.2 %shard_map.50 = (f32[112,128]{1,0:T(8,128)}, f32[416,128]{1,0:T(8,128)}, bf16[416,14336]{1,0:T(8,128)(2,1)}) custom-call(f32[192,192]{1,0:T(8,128)S(1)} %copy-done.1, f32[192,192]{1,0:T(8,128)S(1)} %copy-done.2, f32[192,128]{1,0:T(8,128)S(1)} %copy-done.3, f32[192,416]{1,0:T(8,128)S(1)} %copy-done, ...), custom_call_target="tpu_custom_call" | custom-call | tf_op jit(solution)/shard_map/pallas_call | solution.py:634
Async XLA Ops:
  320.8 1.0 copy-start
  321.8 0.9 copy-start.1
  322.7 0.9 copy-start.2
  323.6 0.9 copy-start.3

commit v6 on v5

--- a/solution.py
+++ b/solution.py
@@ -29,6 +29,14 @@
 STREAMS = ((0, 32, "zyx"), (32, 48, "yxz"), (48, 64, "xzy"))
 RSC, RS, AG, AGC, ARC, ARZ, ARY, ARX, ARB = 0, 1, 10, 19, 20, 21, 22, 23, 24
 EXCHANGES = 25
+
+
+def labels(core, z, y, x):
+    return z + core * (y - z), y + core * (x - y), x + core * (z - x)
+
+
+def chip(core, a, b, c):
+    return a + core * (c - a), b + core * (a - b), c + core * (b - c)
 
 
 def dot(left, right, dims=NN):
@@ -98,19 +106,24 @@
     col_id = lax.axis_index("col")
     y_hi, x = row_id // NX, row_id % NX
     z, y_lo, core = col_id // (NYL * NC), (col_id // NC) % NYL, col_id % NC
-    y = y_hi * NYL + y_lo
+    site = (z, y_hi * NYL + y_lo, x)
+    z, y, x = labels(core, *site)
+    partner_z = labels(1 - core, *site)[0]
     here = {"z": z, "y": y, "x": x}
     sizes = {"c": NC, "z": NZ, "y": ny, "x": NX}
 
+    def device_at(core, z, y, x):
+        return ((y // NYL) * NX + x, (z * NYL + y % NYL) * NC + core)
+
     def device(core, z, y, x):
-        return ((y // NYL) * NX + x, (z * NYL + y % NYL) * NC + core)
+        return device_at(core, *chip(core, z, y, x))
 
     def spot(core, z, y, x):
         return ((core * NZ + z) * ny + y) * NX + x
 
     def peer(axis, d):
         if axis == "c":
-            return device((core + d) % NC, z, y, x)
+            return device_at((core + d) % NC, *site)
         if axis == "z":
             return device(core, (z + d) % NZ, y, x)
         if axis == "y":
@@ -127,7 +140,7 @@
 
     def strip_copy(i):
         dc, dz, dy = offset(i)
-        dr, dl = device((core + dc) % NC, (z + dz) % NZ, (y + dy) % ny, 0)
+        dr, dl = device_at((core + dc) % NC, (site[0] + dz) % NZ, (site[1] + dy) % ny, 0)
         block = dl * (NYH * NX) + dr
         return pltpu.make_async_copy(
             weight_ref.at[:, pl.ds(pl.multiple_of(block * COLS, LANES), NX * COLS)], strip.at[i % 2],
@@ -135,10 +148,10 @@
 
     def block_copy(i, dx):
         dc, dz, dy = offset(i)
-        tx = (x + dx) % NX
+        tx = (site[2] + dx) % NX
         return pltpu.make_async_remote_copy(
             src_ref=staged.at[i, tx], dst_ref=w.at[place, pl.ds(0, SENT)], send_sem=put_sem.at[i, dx], recv_sem=get_sem.at[i, dx],
-            device_id=device((core + dc) % NC, (z + dz) % NZ, (y + dy) % ny, tx), device_id_type=MESH)
+            device_id=device_at((core + dc) % NC, (site[0] + dz) % NZ, (site[1] + dy) % ny, tx), device_id_type=MESH)
 
     strip_copy(0).start()
     barrier = pltpu.get_barrier_semaphore()
@@ -173,7 +186,7 @@
         @pl.when(step == 0)
         def _():
             pl.semaphore_wait(barrier, n - 1)
-            pltpu.make_async_copy(staged.at[0, x], w.at[place, pl.ds(0, SENT)], keep_sem).start()
+            pltpu.make_async_copy(staged.at[0, site[2]], w.at[place, pl.ds(0, SENT)], keep_sem).start()
 
         def rotate(a, _):
             for dx in range(NX):
@@ -263,12 +276,14 @@
     start_low = raw[...].astype(BF16)
     right[0:B, :] = raw[...]
     reduce = Reduce(dot(raw[...], raw[...], NT), 0)
-    pltpu.make_async_copy(staged.at[0, x], w.at[place, pl.ds(0, SENT)], keep_sem).wait()
+    pltpu.make_async_copy(staged.at[0, site[2]], w.at[place, pl.ds(0, SENT)], keep_sem).wait()
 
     def arrive(i, _):
         dc, dz, dy = offset(i)
-        fz, fy = (z - dz + NZ) % NZ, (y - dy + ny) % ny
-        base = spot((core - dc + NC) % NC, fz, fy, 0)
+        source = (core - dc + NC) % NC
+        fz, fy = (site[0] - dz + NZ) % NZ, (site[1] - dy + ny) % ny
+        at = [labels(source, fz, fy, k) for k in range(NX)]
+        spots = [spot(source, *p) for p in at]
         for dx in range(NX):
             if dx == 0:
                 @pl.when(i != 0)
@@ -277,18 +292,19 @@
             else:
                 block_copy(i, dx).wait()
         for k in range(NX):
-            unpack(w, base + k)
-        out = fast(start_low, jnp.concatenate([w[base + k] for k in range(NX)], 1))
+            unpack(w, spots[k])
+        out = fast(start_low, jnp.concatenate([w[p] for p in spots], 1))
 
         @pl.when(dc == 0)
         def _():
             for k in range(NX):
-                acc[(fz * ny + fy) * NX + k] = out[:, k * LANES : (k + 1) * LANES]
+                acc[(at[k][0] * ny + at[k][1]) * NX + at[k][2]] = out[:, k * LANES : (k + 1) * LANES]
 
         @pl.when(dc != 0)
         def _():
             for k in range(NX):
-                core_out[(NZ - dz) % NZ, fy * NX + k] = out[:, k * LANES : (k + 1) * LANES].astype(BF16)
+                core_out[(at[k][0] - partner_z + NZ) % NZ, at[k][1] * NX + at[k][2]] = out[
+                    :, k * LANES : (k + 1) * LANES].astype(BF16)
 
         return 0
 
@@ -313,7 +329,7 @@
         for k in range(PER):
             at = i * PER + k
             r, c = at // (NZ * NYL * NC), at % (NZ * NYL * NC)
-            parts.append(spot(c % NC, c // (NYL * NC), (r // NX) * NYL + (c // NC) % NYL, r % NX))
+            parts.append(spot(c % NC, *labels(c % NC, c // (NYL * NC), (r // NX) * NYL + (c // NC) % NYL, r % NX)))
         for t in range(PER * ROWS // LANES):
             first = w[parts[t]].astype(F32)
             if t:
@@ -344,7 +360,7 @@
             def put(i, value, d=d):
                 core_out[d, i] = value.astype(BF16)
             if j:
-                product_slab(low, base_of(1 - core, (z + d) % NZ), put)
+                product_slab(low, base_of(1 - core, (partner_z + d) % NZ), put)
             core_copies[d] = swap(core_out.at[d], core_in.at[j, d], j, RSC, d)
         if j:
             reduce.step()
@@ -486,7 +502,7 @@
             pltpu.make_async_remote_copy(
                 src_ref=piece, dst_ref=piece, send_sem=send_sem.at[j, AGC, d], recv_sem=recv_sem.at[j, AGC, d],
                 device_id=peer("c", 1), device_id_type=MESH).wait_recv()
-            return back_slab(total, 1 - core, (z + d) % NZ)
+            return back_slab(total, 1 - core, (partner_z + d) % NZ)
 
         total = lax.fori_loop(0, NZ, handed_in, total)
         image, grams = total[:, :COLS], total[:, COLS:]
@@ -601,48 +617,84 @@
     return lax.fori_loop(1, SWEEPS, lambda _, basis: orth(dot(basis, whole)), basis)
 
 
-def finish_kernel(gram_ref, coef_ref, left_ref, image_ref, gathered, weight,
-                  adapter_left, adapter_right, out, high, low, right):
-    @pl.when(pl.program_id(0) == 0)
-    def _():
-        basis = sweeps(gram_ref, coef_ref)
-        adapter_left[...] = dot(basis, left_ref[...]).T[:ROWS]
-        wide = dot(basis, image_ref[...]).T
-        adapter_right[...] = wide
-        right[...] = wide.astype(BF16)
-        mixed = dot(basis, coef_ref[...])
-        high[...] = mixed.astype(BF16)
-        low[...] = (mixed - mixed.astype(BF16).astype(F32)).astype(BF16)
-
-    pieces = []
-    for i in range(PER):
-        at = pl.program_id(0) * PER + i
-        r, c = at // (NZ * NYL * NC), at % (NZ * NYL * NC)
-        place = (c % NC, c // (NYL * NC), (r // NX) * NYL + (c // NC) % NYL, r % NX)
-        pieces.append(jnp.concatenate([gathered[(k,) + place] for k in range(STEPS)], 0))
-    stacked = jnp.concatenate(pieces, 1)
-    left = (fast(high[...], stacked) + fast(low[...], stacked)).astype(BF16).T
-    left = jnp.concatenate([left[i * LANES : i * LANES + ROWS] for i in range(PER)], 0)
-    out[...] = (weight[...].astype(F32) - fast(right[...], left, NT)).astype(BF16)
+def finish_kernel(gram_in, coef_in, left_in, image_in, gathered_in, weight, adapter_left, adapter_right, out,
+                  gram_ref, coef_ref, left_ref, image_ref, gathered, strips, high, low, right,
+                  small_sem, big_sem, load_sem, out_sem):
+    width = PER * ROWS
+    smalls = [pltpu.make_async_copy(src, dst, small_sem.at[i]) for i, (src, dst) in enumerate(
+        ((gram_in, gram_ref), (coef_in, coef_ref), (left_in, left_ref), (image_in, image_ref)))]
+    for copy in smalls:
+        copy.start()
+    big = pltpu.make_async_copy(gathered_in, gathered, big_sem)
+    big.start()
+
+    def place(ref, i):
+        return ref.at[:, pl.ds(pl.multiple_of(i * width, LANES), width)]
+
+    def load(i):
+        return pltpu.make_async_copy(place(weight, i), strips.at[i], load_sem.at[i])
+
+    def store(i):
+        return pltpu.make_async_copy(strips.at[i], place(out, i), out_sem.at[i])
+
+    def each(body):
+        lax.fori_loop(0, strips.shape[0], lambda i, _: (body(i), 0)[1], 0)
+
+    each(lambda i: load(i).start())
+    for copy in smalls:
+        copy.wait()
+    basis = sweeps(gram_ref, coef_ref)
+    adapter_left[...] = dot(basis, left_ref[...]).T[:ROWS]
+    wide = dot(basis, image_ref[...]).T
+    adapter_right[...] = wide
+    right[...] = wide.astype(BF16)
+    mixed = dot(basis, coef_ref[...])
+    high[...] = mixed.astype(BF16)
+    low[...] = (mixed - mixed.astype(BF16).astype(F32)).astype(BF16)
+    big.wait()
+
+    def residual(i):
+        pieces = []
+        for k in range(PER):
+            at = i * PER + k
+            r, c = at // (NZ * NYL * NC), at % (NZ * NYL * NC)
+            core = c % NC
+            where = labels(core, c // (NYL * NC), (r // NX) * NYL + (c // NC) % NYL, r % NX)
+            pieces.append(jnp.concatenate([gathered[(s, core) + where] for s in range(STEPS)], 0))
+        stacked = jnp.concatenate(pieces, 1)
+        left = (fast(high[...], stacked) + fast(low[...], stacked)).astype(BF16).T
+        left = jnp.concatenate([left[k * LANES : k * LANES + ROWS] for k in range(PER)], 0)
+        load(i).wait()
+        strips[i] = (strips[i].astype(F32) - fast(right[...], left, NT)).astype(BF16)
+        store(i).start()
+
+    each(residual)
+    each(lambda i: store(i).wait())
 
 
 def finish(gram, coef, left, images, gathered, blocks):
     rows = blocks.shape[1]
+    n = rows // (PER * ROWS)
     s = STEPS * B
-    whole = lambda shape: pl.BlockSpec(shape, lambda i: (0,) * len(shape))
-    strip = pl.BlockSpec((COLS, PER * ROWS), lambda i: (0, i))
+    vmem = pl.BlockSpec(memory_space=pltpu.VMEM)
+    hbm = pl.BlockSpec(memory_space=pl.ANY)
+    held = [pltpu.VMEM(a.shape, a.dtype) for a in (gram, coef, left, images, gathered)]
     return pl.pallas_call(
         finish_kernel,
-        grid=(rows // (PER * ROWS),),
         out_shape=(
             jax.ShapeDtypeStruct((ROWS, RANK), F32),
             jax.ShapeDtypeStruct((COLS, RANK), F32),
             jax.ShapeDtypeStruct((COLS, rows), BF16),
         ),
-        in_specs=[whole(a.shape) for a in (gram, coef, left, images, gathered)] + [strip],
-        out_specs=(whole((ROWS, RANK)), whole((COLS, RANK)), strip),
-        scratch_shapes=[pltpu.VMEM((RANK, s), BF16), pltpu.VMEM((RANK, s), BF16), pltpu.VMEM((COLS, RANK), BF16)],
-        compiler_params=pltpu.CompilerParams(vmem_limit_bytes=48 * 1024 * 1024),
+        in_specs=[hbm] * 6,
+        out_specs=(vmem, vmem, hbm),
+        scratch_shapes=held + [
+            pltpu.VMEM((n, COLS, PER * ROWS), BF16),
+            pltpu.VMEM((RANK, s), BF16), pltpu.VMEM((RANK, s), BF16), pltpu.VMEM((COLS, RANK), BF16),
+            pltpu.SemaphoreType.DMA((4,)), pltpu.SemaphoreType.DMA, pltpu.SemaphoreType.DMA((n,)),
+            pltpu.SemaphoreType.DMA((n,)),
+        ],
+        compiler_params=pltpu.CompilerParams(vmem_limit_bytes=60 * 1024 * 1024),
     )(gram, coef, left, images, gathered, blocks)
 
 

time: 366 us -> 374 us (1.022)
  Pallas kernels: 360 us -> 372 us
    pallas_call x1, Pallas kernels: 320 us -> 335 us  [chain(): pl.pallas_call(chain_kernel, out_shape=(jax.ShapeDtypeStruct((STEPS, NC,...]
where the time goes in v6:
time: 374 us; the launch traced here: 373 us
  Pallas kernels  372 us (99%)
    pallas_call x1, Pallas kernels, chain(): pl.pallas_call(chain_kernel, out_shape=(jax.ShapeDtypeStruct((STEPS, NC,...  335 us
    pallas_call x1, Pallas kernels, finish(): pl.pallas_call(finish_kernel, out_shape=(jax.ShapeDtypeStruct((ROWS, RANK...  36.8 us

profile of v6, /device:TPU:1, one launch (start us, length us, event | category | flops | bytes accessed | tf_op | source)
XLA Modules:
  0.0 372.6 jit_solution(16428010372971711980)
XLA Ops:
  0.6 334.9 %shard_map.49 = (bf16[3,2,4,4,4,64,128]{6,5,4,3,2,1,0:T(8,128)(2,1)}, f32[192,128]{1,0:T(8,128)}, f32[192,416]{1,0:T(8,128)}, f32[192,192]{1,0:T(8,128)}, f32[19...) custom-call(f32[64,416]{1,0:T(8,128)} %bitcast.2, bf16[112,53248]{1,0:T(8,128)(2,1)} %weight_ref.1), custom_call_target="tpu_custom_call" | custom-call | tf_op jit(solution)/shard_map/pallas_call | solution.py:554
  335.6 36.8 %shard_map.50 = (f32[112,128]{1,0:T(8,128)}, f32[416,128]{1,0:T(8,128)}, bf16[416,14336]{1,0:T(8,128)(2,1)}) custom-call(f32[192,192]{1,0:T(8,128)} %get-tuple-element.12.gram_in, f32[192,192]{1,0:T(8,128)} %get-tuple-element.13.coef_in, f32[192,128]{1,0:T(8,128)} %get-tuple-element.14.left_in, f32[192,416]{1,0:T(8,128)} %get-tuple-element.15.image_in, ...), custom_call_target="tpu_custom_call" | custom-call | tf_op jit(solution)/shard_map/pallas_call | solution.py:682

commit v7 on v6

--- a/solution.py
+++ b/solution.py
@@ -29,14 +29,6 @@
 STREAMS = ((0, 32, "zyx"), (32, 48, "yxz"), (48, 64, "xzy"))
 RSC, RS, AG, AGC, ARC, ARZ, ARY, ARX, ARB = 0, 1, 10, 19, 20, 21, 22, 23, 24
 EXCHANGES = 25
-
-
-def labels(core, z, y, x):
-    return z + core * (y - z), y + core * (x - y), x + core * (z - x)
-
-
-def chip(core, a, b, c):
-    return a + core * (c - a), b + core * (a - b), c + core * (b - c)
 
 
 def dot(left, right, dims=NN):
@@ -106,24 +98,19 @@
     col_id = lax.axis_index("col")
     y_hi, x = row_id // NX, row_id % NX
     z, y_lo, core = col_id // (NYL * NC), (col_id // NC) % NYL, col_id % NC
-    site = (z, y_hi * NYL + y_lo, x)
-    z, y, x = labels(core, *site)
-    partner_z = labels(1 - core, *site)[0]
+    y = y_hi * NYL + y_lo
     here = {"z": z, "y": y, "x": x}
     sizes = {"c": NC, "z": NZ, "y": ny, "x": NX}
 
-    def device_at(core, z, y, x):
+    def device(core, z, y, x):
         return ((y // NYL) * NX + x, (z * NYL + y % NYL) * NC + core)
-
-    def device(core, z, y, x):
-        return device_at(core, *chip(core, z, y, x))
 
     def spot(core, z, y, x):
         return ((core * NZ + z) * ny + y) * NX + x
 
     def peer(axis, d):
         if axis == "c":
-            return device_at((core + d) % NC, *site)
+            return device((core + d) % NC, z, y, x)
         if axis == "z":
             return device(core, (z + d) % NZ, y, x)
         if axis == "y":
@@ -140,7 +127,7 @@
 
     def strip_copy(i):
         dc, dz, dy = offset(i)
-        dr, dl = device_at((core + dc) % NC, (site[0] + dz) % NZ, (site[1] + dy) % ny, 0)
+        dr, dl = device((core + dc) % NC, (z + dz) % NZ, (y + dy) % ny, 0)
         block = dl * (NYH * NX) + dr
         return pltpu.make_async_copy(
             weight_ref.at[:, pl.ds(pl.multiple_of(block * COLS, LANES), NX * COLS)], strip.at[i % 2],
@@ -148,10 +135,10 @@
 
     def block_copy(i, dx):
         dc, dz, dy = offset(i)
-        tx = (site[2] + dx) % NX
+        tx = (x + dx) % NX
         return pltpu.make_async_remote_copy(
             src_ref=staged.at[i, tx], dst_ref=w.at[place, pl.ds(0, SENT)], send_sem=put_sem.at[i, dx], recv_sem=get_sem.at[i, dx],
-            device_id=device_at((core + dc) % NC, (site[0] + dz) % NZ, (site[1] + dy) % ny, tx), device_id_type=MESH)
+            device_id=device((core + dc) % NC, (z + dz) % NZ, (y + dy) % ny, tx), device_id_type=MESH)
 
     strip_copy(0).start()
     barrier = pltpu.get_barrier_semaphore()
@@ -186,7 +173,7 @@
         @pl.when(step == 0)
         def _():
             pl.semaphore_wait(barrier, n - 1)
-            pltpu.make_async_copy(staged.at[0, site[2]], w.at[place, pl.ds(0, SENT)], keep_sem).start()
+            pltpu.make_async_copy(staged.at[0, x], w.at[place, pl.ds(0, SENT)], keep_sem).start()
 
         def rotate(a, _):
             for dx in range(NX):
@@ -276,14 +263,12 @@
     start_low = raw[...].astype(BF16)
     right[0:B, :] = raw[...]
     reduce = Reduce(dot(raw[...], raw[...], NT), 0)
-    pltpu.make_async_copy(staged.at[0, site[2]], w.at[place, pl.ds(0, SENT)], keep_sem).wait()
+    pltpu.make_async_copy(staged.at[0, x], w.at[place, pl.ds(0, SENT)], keep_sem).wait()
 
     def arrive(i, _):
         dc, dz, dy = offset(i)
-        source = (core - dc + NC) % NC
-        fz, fy = (site[0] - dz + NZ) % NZ, (site[1] - dy + ny) % ny
-        at = [labels(source, fz, fy, k) for k in range(NX)]
-        spots = [spot(source, *p) for p in at]
+        fz, fy = (z - dz + NZ) % NZ, (y - dy + ny) % ny
+        base = spot((core - dc + NC) % NC, fz, fy, 0)
         for dx in range(NX):
             if dx == 0:
                 @pl.when(i != 0)
@@ -292,19 +277,18 @@
             else:
                 block_copy(i, dx).wait()
         for k in range(NX):
-            unpack(w, spots[k])
-        out = fast(start_low, jnp.concatenate([w[p] for p in spots], 1))
+            unpack(w, base + k)
+        out = fast(start_low, jnp.concatenate([w[base + k] for k in range(NX)], 1))
 
         @pl.when(dc == 0)
         def _():
             for k in range(NX):
-                acc[(at[k][0] * ny + at[k][1]) * NX + at[k][2]] = out[:, k * LANES : (k + 1) * LANES]
+                acc[(fz * ny + fy) * NX + k] = out[:, k * LANES : (k + 1) * LANES]
 
         @pl.when(dc != 0)
         def _():
             for k in range(NX):
-                core_out[(at[k][0] - partner_z + NZ) % NZ, at[k][1] * NX + at[k][2]] = out[
-                    :, k * LANES : (k + 1) * LANES].astype(BF16)
+                core_out[(NZ - dz) % NZ, fy * NX + k] = out[:, k * LANES : (k + 1) * LANES].astype(BF16)
 
         return 0
 
@@ -329,7 +313,7 @@
         for k in range(PER):
             at = i * PER + k
             r, c = at // (NZ * NYL * NC), at % (NZ * NYL * NC)
-            parts.append(spot(c % NC, *labels(c % NC, c // (NYL * NC), (r // NX) * NYL + (c // NC) % NYL, r % NX)))
+            parts.append(spot(c % NC, c // (NYL * NC), (r // NX) * NYL + (c // NC) % NYL, r % NX))
         for t in range(PER * ROWS // LANES):
             first = w[parts[t]].astype(F32)
             if t:
@@ -360,7 +344,7 @@
             def put(i, value, d=d):
                 core_out[d, i] = value.astype(BF16)
             if j:
-                product_slab(low, base_of(1 - core, (partner_z + d) % NZ), put)
+                product_slab(low, base_of(1 - core, (z + d) % NZ), put)
             core_copies[d] = swap(core_out.at[d], core_in.at[j, d], j, RSC, d)
         if j:
             reduce.step()
@@ -502,7 +486,7 @@
             pltpu.make_async_remote_copy(
                 src_ref=piece, dst_ref=piece, send_sem=send_sem.at[j, AGC, d], recv_sem=recv_sem.at[j, AGC, d],
                 device_id=peer("c", 1), device_id_type=MESH).wait_recv()
-            return back_slab(total, 1 - core, (partner_z + d) % NZ)
+            return back_slab(total, 1 - core, (z + d) % NZ)
 
         total = lax.fori_loop(0, NZ, handed_in, total)
         image, grams = total[:, :COLS], total[:, COLS:]
@@ -659,7 +643,7 @@
             at = i * PER + k
             r, c = at // (NZ * NYL * NC), at % (NZ * NYL * NC)
             core = c % NC
-            where = labels(core, c // (NYL * NC), (r // NX) * NYL + (c // NC) % NYL, r % NX)
+            where = (c // (NYL * NC), (r // NX) * NYL + (c // NC) % NYL, r % NX)
             pieces.append(jnp.concatenate([gathered[(s, core) + where] for s in range(STEPS)], 0))
         stacked = jnp.concatenate(pieces, 1)
         left = (fast(high[...], stacked) + fast(low[...], stacked)).astype(BF16).T

time: 374 us -> 359 us (0.960)
  Pallas kernels: 372 us -> 357 us
    pallas_call x1, Pallas kernels: 335 us -> 320 us  [chain(): pl.pallas_call(chain_kernel, out_shape=(jax.ShapeDtypeStruct((STEPS, NC,...]
where the time goes in v7:
time: 359 us; the launch traced here: 358 us
  Pallas kernels  357 us (99%)
    pallas_call x1, Pallas kernels, chain(): pl.pallas_call(chain_kernel, out_shape=(jax.ShapeDtypeStruct((STEPS, NC,...  320 us
    pallas_call x1, Pallas kernels, finish(): pl.pallas_call(finish_kernel, out_shape=(jax.ShapeDtypeStruct((ROWS, RANK...  36.6 us

profile of v7, /device:TPU:1, one launch (start us, length us, event | category | flops | bytes accessed | tf_op | source)
XLA Modules:
  0.0 357.5 jit_solution(6133178888020204379)
XLA Ops:
  0.6 320.1 %shard_map.49 = (bf16[3,2,4,4,4,64,128]{6,5,4,3,2,1,0:T(8,128)(2,1)}, f32[192,128]{1,0:T(8,128)}, f32[192,416]{1,0:T(8,128)}, f32[192,192]{1,0:T(8,128)}, f32[19...) custom-call(f32[64,416]{1,0:T(8,128)} %bitcast.2, bf16[112,53248]{1,0:T(8,128)(2,1)} %weight_ref.1), custom_call_target="tpu_custom_call" | custom-call | tf_op jit(solution)/shard_map/pallas_call | solution.py:538
  320.8 36.6 %shard_map.50 = (f32[112,128]{1,0:T(8,128)}, f32[416,128]{1,0:T(8,128)}, bf16[416,14336]{1,0:T(8,128)(2,1)}) custom-call(f32[192,192]{1,0:T(8,128)} %get-tuple-element.12.gram_in, f32[192,192]{1,0:T(8,128)} %get-tuple-element.13.coef_in, f32[192,128]{1,0:T(8,128)} %get-tuple-element.14.left_in, f32[192,416]{1,0:T(8,128)} %get-tuple-element.15.image_in, ...), custom_call_target="tpu_custom_call" | custom-call | tf_op jit(solution)/shard_map/pallas_call | solution.py:666
